TPU v7x, 128 devices: a whole 4x4x4 slice. The times are simulated.
128 devices in a mesh: dp: 8 (over z, core), tensor: 16 (over x, y).
Axes of the slice: x: 4, y: 4, z: 4, core: 2. Of those that a mesh axis runs over, the one named last changes fastest.
Arguments:
- activations: bfloat16 [8, 1024, 5120], P('dp'), may hold values from -6 to 6
- out_grad_q: bfloat16 [8, 1024, 5120], P('dp', None, 'tensor'), may hold values from -0.1875 to 0.1875
- out_grad_kv: bfloat16 [8, 1024, 2048], P('dp', None, 'tensor'), may hold values from -0.1875 to 0.1875
- error_q: bfloat16 [8, 5120, 5120], P('dp', None, 'tensor'), may hold values from -4 to 4
- error_kv: bfloat16 [8, 5120, 2048], P('dp', None, 'tensor'), may hold values from -4 to 4
- basis_q: float32 [5120, 32], P('tensor'), may hold values from -0.078125 to 0.078125
- basis_kv: float32 [2048, 32], P('tensor'), may hold values from -0.125 to 0.125
Outputs:
- update_q: bfloat16 [5120, 5120], P(None, 'tensor')
- update_kv: bfloat16 [5120, 2048], P(None, 'tensor')
- error_q_next: bfloat16 [8, 5120, 5120], P('dp', None, 'tensor')
- error_kv_next: bfloat16 [8, 5120, 2048], P('dp', None, 'tensor')
- basis_q_next: float32 [5120, 32], P('tensor')
- basis_kv_next: float32 [2048, 32], P('tensor')
All inputs are finite; a program needn't handle non-finite values.
Results may differ from a plain program's by a relative error of at most 0.0012.
Values sent between devices are 32-bit elements; how exact they have to be, the bound alone decides.
A program may use at most 128 MiB of HBM per device.

v0:
```python
import jax
import jax.numpy as jnp
from jax import lax
from jax.sharding import PartitionSpec as P


def weight_grad(activations, out_grad, error):
    grads = lax.dot_general(
        activations[0], out_grad[0], (((0,), (0,)), ((), ())), preferred_element_type=jnp.float32
    )
    return grads + error[0].astype(jnp.float32)


def make_gram(left):
    return jnp.dot(left.T, left, precision=lax.Precision.HIGHEST)


def orthonormal(left, gram):
    lower = jnp.linalg.cholesky(gram)
    return lax.linalg.triangular_solve(lower, left, left_side=False, lower=True, transpose_a=True)


def local(activations, out_grad_q, out_grad_kv, error_q, error_kv, basis_q, basis_kv):
    rank_cols = basis_q.shape[1]
    full_q = weight_grad(activations, out_grad_q, error_q)
    full_kv = weight_grad(activations, out_grad_kv, error_kv)
    local_left = jnp.concatenate(
        [
            jnp.dot(full_q, basis_q, precision=lax.Precision.HIGHEST),
            jnp.dot(full_kv, basis_kv, precision=lax.Precision.HIGHEST),
        ],
        axis=1,
    )
    left_both = lax.psum(local_left, ("dp", "tensor"))
    left_q = left_both[:, :rank_cols]
    left_kv = left_both[:, rank_cols:]
    ortho_q = orthonormal(left_q, make_gram(left_q))
    ortho_kv = orthonormal(left_kv, make_gram(left_kv))
    local_q = lax.dot_general(
        full_q, ortho_q, (((0,), (0,)), ((), ())), precision=lax.Precision.HIGHEST
    )
    local_kv = lax.dot_general(
        full_kv, ortho_kv, (((0,), (0,)), ((), ())), precision=lax.Precision.HIGHEST
    )
    summed_q, summed_kv = lax.psum((local_q, local_kv), "dp")
    replica_count = lax.axis_size("dp")
    basis_q_next = summed_q / replica_count
    basis_kv_next = summed_kv / replica_count
    approx_q = jnp.dot(ortho_q, basis_q_next.T, precision=lax.Precision.HIGHEST)
    approx_kv = jnp.dot(ortho_kv, basis_kv_next.T, precision=lax.Precision.HIGHEST)
    update_q = approx_q.astype(jnp.bfloat16)
    update_kv = approx_kv.astype(jnp.bfloat16)
    error_q_next = (full_q - approx_q)[None].astype(jnp.bfloat16)
    error_kv_next = (full_kv - approx_kv)[None].astype(jnp.bfloat16)
    return (update_q, update_kv, error_q_next, error_kv_next, basis_q_next, basis_kv_next)


def solution(mesh):
    placed = (
        P("dp", None, None),
        P("dp", None, "tensor"),
        P("dp", None, "tensor"),
        P("dp", None, "tensor"),
        P("dp", None, "tensor"),
        P("tensor", None),
        P("tensor", None),
    )
    return jax.shard_map(
        local,
        mesh=mesh,
        in_specs=placed,
        out_specs=(
            P(None, "tensor"),
            P(None, "tensor"),
            P("dp", None, "tensor"),
            P("dp", None, "tensor"),
            P("tensor", None),
            P("tensor", None),
        ),
        check_vma=False,
    )
```

profile of v0, /device:TPU:1, one launch (start us, length us, event | category | flops | bytes accessed | tf_op | source)
XLA Modules:
  0.0 256.2 jit_solution(15992159277112201822)
XLA Ops:
  7.2 0.0 copy-start
  7.2 0.0 copy-start.11
  7.2 0.0 all-reduce.3.cloned.1.call-start
  7.2 1.0 copy-done
  8.3 8.6 %fusion.4 = f32[5120,320]{0,1:T(8,128)S(1)} fusion(bf16[1,1024,5120]{2,1,0:T(8,128)(2,1)} %param.10, bf16[1,5120,320]{1,2,0:T(8,128)(2,1)} %param.13, bf16[1,1024,320]{1,2,0:T(8,128)(2,1)S(1)} %copy-done), kind=kOutput, calls=%fused_computation.4 | convolution fusion | flops 3358720000 | bytes 20971520 | tf_op jit(solution)/shard_map/dot_general | solution.py:8
  16.9 0.0 copy-done.11
  16.9 0.0 copy-start.1
  16.9 0.0 copy-start.7
  16.9 0.0 copy-start.8
  16.9 4.2 %fusion.26 = f32[5120,32]{0,1:T(8,128)S(1)} fusion(f32[5120,320]{0,1:T(8,128)S(1)} %fusion.4, f32[320,32]{0,1:T(8,128)S(1)} %copy-done.11), kind=kOutput, calls=%fused_computation.39 | convolution fusion | flops 629145600 | bytes 7249920 | tf_op jit(solution)/shard_map/dot_general | solution.py:29
  21.1 0.0 copy-done.1
  21.1 0.0 copy-done.2
  21.1 0.0 copy-done.7
  21.1 0.0 copy-done.8
  21.1 0.0 copy-start.12
  21.2 3.0 %fusion.7 = f32[5120,128]{1,0:T(8,128)S(1)} fusion(bf16[1,1024,5120]{2,1,0:T(8,128)(2,1)S(1)} %copy-done.2, bf16[1,5120,128]{2,1,0:T(8,128)(2,1)S(1)} %copy-done.7, bf16[1,1024,128]{2,1,0:T(8,128)(2,1)S(1)} %copy-done.8), kind=kOutput, calls=%fused_computation.6 | convolution fusion | flops 1343488000 | bytes 14680064 | tf_op jit(solution)/shard_map/dot_general | solution.py:8
  24.2 0.0 copy-done.12
  24.2 2.7 %fusion.27 = f32[5120,32]{0,1:T(8,128)S(1)} fusion(f32[5120,128]{1,0:T(8,128)S(1)} %fusion.7, f32[128,32]{0,1:T(8,128)S(1)} %copy-done.12), kind=kOutput, calls=%fused_computation.40 | convolution fusion | flops 251658240 | bytes 3293184 | tf_op jit(solution)/shard_map/dot_general | solution.py:30
  26.9 1.1 pad_maximum_fusion
  28.0 0.0 all-reduce.3.cloned.1.call-update
  28.1 151.4 %all-reduce.3.cloned.1.call-done = f32[5120,64]{0,1:T(8,128)} async-done(((f32[5120,64]{0,1:T(8,128)}), f32[5120,64]{0,1:T(8,128)}) %all-reduce.3.cloned.1.call-update) | async-done | bytes 1310736 | tf_op jit(solution)/shard_map/psum | solution.py:34
  179.5 1.9 fusion.14
  181.4 0.1 copy.14
  181.5 3.0 %cholesky.55 = f32[32,32]{1,0:T(8,128)S(1)} custom-call(f32[32,32]{1,0:T(8,128)S(1)} %fusion.23), custom_call_target="Cholesky" | custom-call | tf_op jit(solution)/shard_map/jit(cholesky)/cholesky | solution.py:19
  184.6 0.6 compare_reduce_fusion
  185.2 0.7 fusion.21
  185.9 2.4 custom-call.7
  188.3 1.9 convolution_bitcast_fusion
  190.2 0.0 copy-start.5
  190.3 0.8 copy-done.5
  191.1 1.7 fusion.29
  192.8 0.7 fusion.17
  193.4 0.1 copy.13
  193.5 2.9 %cholesky.44 = f32[32,32]{1,0:T(8,128)S(1)} custom-call(f32[32,32]{1,0:T(8,128)S(1)} %fusion.25), custom_call_target="Cholesky" | custom-call | tf_op jit(solution)/shard_map/jit(cholesky)/cholesky | solution.py:19
  196.4 0.6 compare_reduce_fusion.1
  197.1 0.7 fusion.20
  197.8 2.4 custom-call.6
  200.2 1.8 convolution_bitcast_fusion.1
  202.0 0.0 copy-start.3
  202.0 0.8 copy-done.3
  202.9 7.5 %fusion.28 = f32[320,32]{0,1:T(8,128)S(1)} fusion(f32[5120,320]{0,1:T(8,128)} %copy-done.1, f32[5120,32]{0,1:T(8,128)S(1)} %convolution_bitcast_fusion.1), kind=kOutput, calls=%fused_computation.41 | convolution fusion | flops 629145600 | bytes 7249920 | tf_op jit(solution)/shard_map/dot_general | solution.py:39
  210.3 22.7 %all-reduce = (f32[320,32]{0,1:T(8,128)S(1)}, f32[128,32]{0,1:T(8,128)S(1)}) all-reduce(f32[320,32]{0,1:T(8,128)S(1)} %fusion.28, f32[128,32]{0,1:T(8,128)S(1)} %fusion.29), channel_id=1, replica_groups=mesh['dp'=8,'tensor'=16] {'dp'}, use_global_device_ids=true, to_apply=%region_3.6 | all-reduce | flops 14336 | bytes 114688 | tf_op jit(solution)/shard_map/psum | solution.py:45
  233.1 0.0 copy-start.10
  233.1 0.0 copy-start.4
  233.1 6.9 %fusion.11 = (bf16[1,5120,128]{2,1,0:T(8,128)(2,1)}, bf16[5120,128]{1,0:T(8,128)(2,1)}) fusion(f32[5120,128]{1,0:T(8,128)S(1)} %fusion.7, f32[5120,32]{0,1:T(8,128)} %copy-done.5, f32[128,32]{0,1:T(8,128)S(1)} %broadcast_multiply_fusion.1), kind=kOutput, calls=%fused_computation.11 | convolution fusion | flops 253624320 | bytes 5914624 | tf_op jit(solution)/shard_map/dot_general | solution.py:50
  240.0 0.0 copy-start.9
  240.0 9.3 %fusion.10 = (bf16[1,5120,320]{1,2,0:T(8,128)(2,1)}, bf16[5120,320]{0,1:T(8,128)(2,1)}) fusion(f32[5120,320]{0,1:T(8,128)} %copy-done.1, f32[5120,32]{0,1:T(8,128)S(1)} %copy-done.4, f32[320,32]{0,1:T(8,128)S(1)} %broadcast_multiply_fusion), kind=kOutput, calls=%fused_computation.9 | convolution fusion | flops 634060800 | bytes 13803520 | tf_op jit(solution)/shard_map/dot_general | solution.py:49
  249.4 0.0 copy-done.9
  (11 shorter events, 0.1 us)
Async XLA Ops:
  7.2 1.1 copy-start
  7.2 9.7 %copy-start.11 = (f32[320,32]{0,1:T(8,128)S(1)}, f32[320,32]{0,1:T(8,128)}, u32[]{:S(2)}) copy-start(f32[320,32]{0,1:T(8,128)} %param.15) | copy-start | bytes 122884
  7.2 172.3 %all-reduce.3.cloned.1.call-start = ((), (), s32[]{:S(2)}) async-start(), calls=%async_computation | async-start | bytes 2621440 | tf_op jit(solution)/shard_map/psum | solution.py:34
  8.3 12.9 %copy-start.2 = (bf16[1,1024,5120]{2,1,0:T(8,128)(2,1)S(1)}, bf16[1,1024,5120]{2,1,0:T(8,128)(2,1)}, u32[]{:S(2)}) copy-start(bf16[1,1024,5120]{2,1,0:T(8,128)(2,1)} %param.10) | copy-start | bytes 31457284
  16.9 4.2 %copy-start.1 = (f32[5120,320]{0,1:T(8,128)}, f32[5120,320]{0,1:T(8,128)S(1)}, u32[]{:S(2)}) copy-start(f32[5120,320]{0,1:T(8,128)S(1)} %fusion.4) | copy-start | bytes 19660804
  16.9 4.2 %copy-start.7 = (bf16[1,5120,128]{2,1,0:T(8,128)(2,1)S(1)}, bf16[1,5120,128]{2,1,0:T(8,128)(2,1)}, u32[]{:S(2)}) copy-start(bf16[1,5120,128]{2,1,0:T(8,128)(2,1)} %param.14) | copy-start | bytes 3932164
  16.9 4.2 %copy-start.8 = (bf16[1,1024,128]{2,1,0:T(8,128)(2,1)S(1)}, bf16[1,1024,128]{2,1,0:T(8,128)(2,1)}, u32[]{:S(2)}) copy-start(bf16[1,1024,128]{2,1,0:T(8,128)(2,1)} %param.12) | copy-start | bytes 786436
  21.1 3.0 %copy-start.12 = (f32[128,32]{0,1:T(8,128)S(1)}, f32[128,32]{0,1:T(8,128)}, u32[]{:S(2)}) copy-start(f32[128,32]{0,1:T(8,128)} %param.16) | copy-start | bytes 49156
  188.3 4.4 %copy-start.6 = (f32[5120,64]{0,1:T(8,128)S(1)}, f32[5120,64]{0,1:T(8,128)}, u32[]{:S(2)}) copy-start(f32[5120,64]{0,1:T(8,128)} %all-reduce.3.cloned.1.call-done) | copy-start | bytes 3932164
  190.2 0.8 copy-start.5
  202.0 0.8 copy-start.3
  233.1 6.9 %copy-start.10 = (f32[128,32]{0,1:T(8,128)}, f32[128,32]{0,1:T(8,128)S(1)}, u32[]{:S(2)}) copy-start(f32[128,32]{0,1:T(8,128)S(1)} %broadcast_multiply_fusion.1) | copy-start | bytes 49156
  233.1 6.9 %copy-start.4 = (f32[5120,32]{0,1:T(8,128)S(1)}, f32[5120,32]{0,1:T(8,128)}, u32[]{:S(2)}) copy-start(f32[5120,32]{0,1:T(8,128)} %copy-done.3) | copy-start | bytes 1966084
  240.0 9.3 %copy-start.9 = (f32[320,32]{0,1:T(8,128)}, f32[320,32]{0,1:T(8,128)S(1)}, u32[]{:S(2)}) copy-start(f32[320,32]{0,1:T(8,128)S(1)} %broadcast_multiply_fusion) | copy-start | bytes 122884
Sparse Core Ops, SparseCore 0:
  28.2 151.2 all-reduce.2
where the time goes:
time: 259 us; the launch traced here: 256 us
  waiting for transfers between devices  151 us (58%)
  matrix products  50.2 us (19%)
  blocking collectives  22.7 us (9%)
  other arithmetic  14.6 us (6%)
  between operations  14.3 us (6%)
  local copies, waits for them, and re-layouts  2.89 us (1%)
    psum x1, waiting for transfers between devices, local(): left_both = lax.psum(local_left, ('dp', 'tensor'))  151 us
    psum x1, blocking collectives, local(): summed_q, summed_kv = lax.psum((local_q, local_kv), 'dp')  22.7 us
    dot_general x2, matrix products, weight_grad(): lax.dot_general(activations[0], out_grad[0], (((0,), (0,)), ((), ())), pr...  11.6 us
    dot_general x1, matrix products, local(): approx_q = jnp.dot(ortho_q, basis_q_next.T, precision=lax.Precision.HIGHEST)  9.33 us
    dot_general x1, matrix products, local(): lax.dot_general(full_q, ortho_q, (((0,), (0,)), ((), ())), precision=lax....  7.46 us
    another operation x6, other arithmetic, orthonormal(): lower = jnp.linalg.cholesky(gram)  7.29 us
    dot_general x1, matrix products, local(): jnp.dot(ortho_kv, basis_kv_next.T, precision=lax.Precision.HIGHEST)  6.89 us
    another operation x4, other arithmetic, orthonormal(): lax.linalg.triangular_solve(lower, left, left_side=False, lower=True, tra...  6.17 us
  transfers between devices with their start and end apart: 1, of which 1 were waited for; matrix products, arithmetic and copies ran while one was open for 0% of the time, Pallas kernels for 0%

commit v1 on v0

v1 whole, which is shorter than its diff:
```python
import functools

import jax
import jax.numpy as jnp
from jax import lax
from jax.experimental import pallas as pl
from jax.experimental.pallas import tpu as pltpu
from jax.sharding import PartitionSpec as P

F32 = jnp.float32
BF16 = jnp.bfloat16
MESH = pl.DeviceIdType.MESH
HIGHEST = lax.Precision.HIGHEST
MIB = 1 << 20

SIDE = 4
D = 5120
QUART = D // SIDE
TOK = 1024
CQ, CKV = 320, 128
COLS = CQ + CKV
RANK = 32
WIDE = 512
SUB = 640
ROT = (1, 2, 3, 0)
AG_ORDER = (0, 1, 3, 2)


def mm(a, b):
    return jnp.dot(a, b, preferred_element_type=F32)


def mm_t(a, b, precision=None):
    return lax.dot_general(a, b, (((1,), (1,)), ((), ())), preferred_element_type=F32, precision=precision)


def tmm(a, b, precision=None):
    return lax.dot_general(a, b, (((0,), (0,)), ((), ())), preferred_element_type=F32, precision=precision)


def halves(v):
    high = v.astype(BF16)
    return high, (v - high.astype(F32)).astype(BF16)


def eliminate(a, off):
    row = lax.broadcasted_iota(jnp.int32, (RANK, 128), 0)
    lane = lax.broadcasted_iota(jnp.int32, (RANK, 128), 1)
    for k in range(RANK - 1):
        col = jnp.broadcast_to(a[:, off + k : off + k + 1], (RANK, 128))
        scaled = a[k : k + 1, :] / col[k : k + 1, :]
        a = a - jnp.where(row > k, col, 0.0) * scaled
    diag = jnp.sum(jnp.where(lane == row + off, a, 0.0), axis=1, keepdims=True)
    return a * lax.rsqrt(diag)


def reduce_kernel(
    act, ogq, ogkv, eq, ekv, bq, bkv,
    fqh_o, fqm_o, fkv_o, lq_o, tkv_o, zq_o, zkv_o, bn_o,
    act_v, ogkv_v, og_v, eq_v, ekv_v, bq_v, bkv_v, pst_v, bq2_v, bkv2_v,
    loc_v, xr_v, sum_v, rs_buf, zbuf, lt_v, lst_v, lq_v, tkv_v, fqh_v, fqm_v, fkv_v,
    yloc_v, yx_v, yz_v, ysum_v, gram_v, zq_v, zkv_v, bn_v,
    ld, lda, xs, xr, rs_s, rs_r, zs, zr, ag_s, ag_r, fw_s, fw_r, y_s, y_r, out_s,
):
    dp, t = lax.axis_index("dp"), lax.axis_index("tensor")
    z, c = dp // 2, lax.rem(dp, 2)
    x, y = t // SIDE, lax.rem(t, SIDE)
    partner = (z * 2 + 1 - c, t)

    def plane(dx, dy):
        return (dp, lax.rem(x + dx, SIDE) * SIDE + lax.rem(y + dy, SIDE))

    def along_z(dz):
        return (lax.rem(z + dz, SIDE) * 2 + c, t)

    chunks = [lax.rem(x + dx, SIDE) for dx in ROT]

    first = [
        pltpu.make_async_copy(src, dst, ld.at[i])
        for i, (src, dst) in enumerate(
            [(ogq.at[0], og_v.at[pl.ds(CKV, CQ), :]), (ogkv.at[0], ogkv_v), (bq, bq_v), (bkv, bkv_v)]
        )
    ]
    for cp in first:
        cp.start()
    loads = []
    for k, g in enumerate(chunks):
        at = pl.ds(pl.multiple_of(g * QUART, QUART), QUART)
        cps = [
            pltpu.make_async_copy(act.at[0, :, at], act_v.at[g], lda.at[k, 0]),
            pltpu.make_async_copy(eq.at[0, :, at], eq_v.at[g], lda.at[k, 1]),
            pltpu.make_async_copy(ekv.at[0, at, :], ekv_v.at[g], lda.at[k, 2]),
        ]
        for cp in cps:
            cp.start()
        loads.append(cps)

    barrier = pltpu.get_barrier_semaphore()
    peers = [partner]
    peers += [plane(dx, dy) for dx in range(SIDE) for dy in range(SIDE) if dx or dy]
    peers += [along_z(dz) for dz in (1, 2, 3)]
    for p in peers:
        pl.semaphore_signal(barrier, inc=1, device_id=p, device_id_type=MESH)

    for cp in first:
        cp.wait()
    og_v[:CKV, :] = jnp.transpose(ogkv_v[...])
    for src, b2, og_rows, base in ((bq_v, bq2_v, slice(CKV, COLS), 0), (bkv_v, bkv2_v, slice(0, CKV), 2 * RANK)):
        bt = src[...]
        high, mid = halves(bt)
        low = (bt - high.astype(F32) - mid.astype(F32)).astype(BF16)
        b2[:RANK, :] = high
        b2[RANK:, :] = mid
        og_w = og_v[og_rows, :]
        proj = mm(high, og_w) + (mm(mid, og_w) + mm(low, og_w))
        p_high, p_mid = halves(proj)
        pst_v[base : base + RANK, :] = p_high
        pst_v[base + RANK : base + 2 * RANK, :] = p_mid

    def exchange(k):
        theirs = pl.ds(pl.multiple_of((1 - c) * RANK, RANK), RANK)
        return pltpu.make_async_remote_copy(
            src_ref=loc_v.at[k, theirs, :], dst_ref=xr_v.at[k], send_sem=xs.at[k], recv_sem=xr.at[k],
            device_id=partner, device_id_type=MESH,
        )

    def scatter(k):
        exchange(k).wait()
        mine = pl.ds(pl.multiple_of(c * RANK, RANK), RANK)
        sum_v[k] = loc_v[k, mine, :] + xr_v[k]
        for dy in range(SIDE):
            if ROT[k] or dy:
                rows = pl.ds(pl.multiple_of(lax.rem(y + dy, SIDE) * 8, 8), 8)
                pltpu.make_async_remote_copy(
                    src_ref=sum_v.at[k, rows, :], dst_ref=rs_buf.at[ROT[k] * SIDE + dy - 1],
                    send_sem=rs_s, recv_sem=rs_r,
                    device_id=plane(ROT[k], dy), device_id_type=MESH,
                ).start()

    for k, g in enumerate(chunks):
        for cp in loads[k]:
            cp.wait()
        bq2, bkv2 = bq2_v[...], bkv2_v[...]
        pst = pst_v[...]
        for i in range(QUART // 256):
            cut = slice(i * 256, (i + 1) * 256)
            prod = mm(pst, act_v[g, :, cut])
            from_q = mm(bq2, eq_v[g, :, cut])
            from_kv = mm_t(bkv2, ekv_v[g, cut, :])
            loc_v[k, :RANK, cut] = (prod[:RANK] + prod[RANK : 2 * RANK]) + (from_q[:RANK] + from_q[RANK:])
            loc_v[k, RANK:, cut] = (prod[2 * RANK : 3 * RANK] + prod[3 * RANK :]) + (from_kv[:RANK] + from_kv[RANK:])
        if k == 0:
            pl.semaphore_wait(barrier, len(peers))
        exchange(k).start()
        if k >= 1:
            scatter(k - 1)
    scatter(SIDE - 1)

    def gradient(lo, hi):
        def body(i, _):
            g, j = i // (QUART // SUB), lax.rem(i, QUART // SUB)
            at = pl.ds(pl.multiple_of(j * SUB, SUB), SUB)
            grads = mm(og_v[...], act_v[g, :, at])
            high, mid = halves(jnp.transpose(grads[:CKV]) + ekv_v[g, at, :].astype(F32))
            fkv_v[g, at, :CKV] = high
            fkv_v[g, at, CKV:] = mid
            high, mid = halves(grads[CKV:] + eq_v[g, :, at].astype(F32))
            fqh_v[g, :, at] = high
            fqm_v[g, :, at] = mid
            return 0

        lax.fori_loop(lo, hi, body, 0)

    gradient(0, 5)

    pltpu.make_async_copy(rs_buf, rs_buf, rs_r).wait()
    own = pl.ds(pl.multiple_of(y * 8, 8), 8)
    part = sum_v[SIDE - 1, own, :]
    for o in range(SIDE * SIDE - 1):
        part = part + rs_buf[o]
    zbuf[z] = part
    for dz in (1, 2, 3):
        pltpu.make_async_remote_copy(
            src_ref=zbuf.at[z], dst_ref=zbuf.at[z], send_sem=zs, recv_sem=zr,
            device_id=along_z(dz), device_id_type=MESH,
        ).start()

    gradient(5, 8)

    three = zbuf.at[pl.ds(0, 3)]
    pltpu.make_async_copy(three, three, zr).wait()
    at = pl.ds(pl.multiple_of(c * RANK + y * 8, 8), 8)
    lt_v[x, at, :] = (zbuf[0] + zbuf[1]) + (zbuf[2] + zbuf[3])
    for dx in range(SIDE):
        for dy in range(SIDE):
            if dx or dy:
                pltpu.make_async_remote_copy(
                    src_ref=lt_v.at[x, at, :], dst_ref=lt_v.at[x, at, :], send_sem=ag_s, recv_sem=ag_r.at[x],
                    device_id=plane(dx, dy), device_id_type=MESH,
                ).start()

    outs = []
    for g in range(SIDE):
        at = pl.ds(g * QUART, QUART)
        outs.append(pltpu.make_async_copy(fqh_v.at[g], fqh_o.at[:, at], out_s.at[0, g]))
        outs.append(pltpu.make_async_copy(fqm_v.at[g], fqm_o.at[:, at], out_s.at[1, g]))
        outs.append(pltpu.make_async_copy(fkv_v.at[g], fkv_o.at[at, :], out_s.at[2, g]))
    for cp in outs:
        cp.start()

    mine = pl.ds(pl.multiple_of(c * RANK, RANK), RANK)

    def forward(i):
        g = lax.rem(x + AG_ORDER[i], SIDE)
        return pltpu.make_async_remote_copy(
            src_ref=lt_v.at[g, mine, :], dst_ref=lt_v.at[g, mine, :], send_sem=fw_s.at[i], recv_sem=fw_r.at[i],
            device_id=partner, device_id_type=MESH,
        )

    accs = [jnp.zeros((CQ, 2 * RANK), F32), jnp.zeros((CQ, RANK), F32), jnp.zeros((2 * RANK, 2 * CKV), F32)]

    def term(i, accs):
        forward(i).wait()
        g = lax.rem(x + AG_ORDER[i], SIDE)
        high, mid = halves(lt_v[g])
        lst_v[g, :RANK, :] = high[:RANK]
        lst_v[g, RANK : 2 * RANK, :] = mid[:RANK]
        lst_v[g, 2 * RANK : 3 * RANK, :] = high[RANK:]
        lst_v[g, 3 * RANK :, :] = mid[RANK:]
        return [
            accs[0] + mm_t(fqh_v[g], lst_v[g, : 2 * RANK, :]),
            accs[1] + mm_t(fqm_v[g], lst_v[g, :RANK, :]),
            accs[2] + mm(lst_v[g, 2 * RANK :, :], fkv_v[g]),
        ]

    for i, dx in enumerate(AG_ORDER):
        g = lax.rem(x + dx, SIDE)
        got = rs_buf.at[pl.ds(0, SIDE if dx else SIDE - 1)]
        pltpu.make_async_copy(got, got, ag_r.at[g]).wait()
        forward(i).start()
        if i >= 1:
            accs = term(i - 1, accs)
    accs = term(SIDE - 1, accs)

    by_high = jnp.transpose(accs[0])
    yloc_v[:, CKV:COLS] = by_high[:RANK] + (by_high[RANK:] + jnp.transpose(accs[1]))
    yloc_v[:, :CKV] = accs[2][:RANK, :CKV] + (accs[2][RANK:, :CKV] + accs[2][:RANK, CKV:])
    yloc_v[:, COLS:] = jnp.zeros((RANK, WIDE - COLS), F32)

    my_rows = pl.ds(pl.multiple_of(c * 16, 16), 16)
    their_rows = pl.ds(pl.multiple_of((1 - c) * 16, 16), 16)
    cp = pltpu.make_async_remote_copy(
        src_ref=yloc_v.at[their_rows, :], dst_ref=yx_v, send_sem=y_s.at[0], recv_sem=y_r.at[0],
        device_id=partner, device_id_type=MESH,
    )
    cp.start()
    cp.wait()
    yz_v[z] = yloc_v[my_rows, :] + yx_v[...]
    for dz in (1, 2, 3):
        pltpu.make_async_remote_copy(
            src_ref=yz_v.at[z], dst_ref=yz_v.at[z], send_sem=y_s.at[1], recv_sem=y_r.at[1],
            device_id=along_z(dz), device_id_type=MESH,
        ).start()

    gram = jnp.zeros((2 * RANK, 2 * RANK), F32)
    for g in range(SIDE):
        full = lt_v[g]
        gram = gram + mm_t(full, full, precision=HIGHEST)
    gram_v[:, : 2 * RANK] = gram
    row = lax.broadcasted_iota(jnp.int32, (2 * RANK, 128), 0)
    lane = lax.broadcasted_iota(jnp.int32, (2 * RANK, 128), 1)
    gram_v[:, 2 * RANK :] = jnp.zeros((2 * RANK, 2 * RANK), F32)
    same = (row < RANK) == (lane < RANK)
    aug = jnp.where(lane < 2 * RANK, jnp.where(same, gram_v[...], 0.0), jnp.where(lane == row + 2 * RANK, 1.0, 0.0))
    inv_q = eliminate(aug[:RANK], 0)
    inv_kv = eliminate(aug[RANK:], RANK)
    gram_v[:RANK, :] = inv_q
    gram_v[RANK:, :] = inv_kv
    inv = gram_v[:, 2 * RANK :]
    left_copies = []
    for g in range(SIDE):
        lq_v[g, : 2 * RANK, :] = lst_v[g, : 2 * RANK, :]
        lq_v[g, 2 * RANK :, :] = lst_v[g, : 2 * RANK, :]
        kv = lst_v[g, 2 * RANK :, :]
        tkv_v[g] = jnp.transpose(jnp.concatenate([kv, kv], axis=0))
        at = pl.ds(g * QUART, QUART)
        left_copies.append(pltpu.make_async_copy(lq_v.at[g], lq_o.at[:, at], out_s.at[3, g]))
        left_copies.append(pltpu.make_async_copy(tkv_v.at[g], tkv_o.at[at, :], out_s.at[4, g]))
    for cp in left_copies:
        cp.start()

    three = yz_v.at[pl.ds(0, 3)]
    pltpu.make_async_copy(three, three, y_r.at[1]).wait()
    ysum_v[my_rows, :] = (yz_v[0] + yz_v[1]) + (yz_v[2] + yz_v[3])
    cp = pltpu.make_async_remote_copy(
        src_ref=ysum_v.at[my_rows, :], dst_ref=ysum_v.at[my_rows, :], send_sem=y_s.at[2], recv_sem=y_r.at[2],
        device_id=partner, device_id_type=MESH,
    )
    cp.start()
    cp.wait()

    total = ysum_v[...]
    is_kv = lax.broadcasted_iota(jnp.int32, (RANK, WIDE), 1) < CKV
    both = jnp.concatenate([jnp.where(is_kv, 0.0, total), jnp.where(is_kv, total, 0.0)], axis=0)
    new_t = jnp.dot(inv, both, precision=HIGHEST, preferred_element_type=F32) * (1.0 / 8.0)
    factor = tmm(inv, new_t, precision=HIGHEST)
    bn_v[...] = new_t[:RANK] + new_t[RANK:]
    high, mid = halves(factor)
    stack = jnp.concatenate([high[:RANK], high[:RANK], mid[:RANK], mid[:RANK]], axis=0)
    zq_v[...] = jnp.transpose(stack[:, CKV:COLS])
    zkv_v[...] = jnp.concatenate([high[RANK:], high[RANK:], mid[RANK:], mid[RANK:]], axis=0)[:, :CKV]
    last = [
        pltpu.make_async_copy(zq_v, zq_o, ld.at[0]),
        pltpu.make_async_copy(zkv_v, zkv_o, ld.at[1]),
        pltpu.make_async_copy(bn_v, bn_o, ld.at[2]),
    ]
    for cp in last:
        cp.start()

    pltpu.make_async_copy(rs_buf, rs_buf, rs_s).wait()
    three = zbuf.at[pl.ds(0, 3)]
    pltpu.make_async_copy(three, three, zs).wait()
    pltpu.make_async_copy(rs_buf, rs_buf, ag_s).wait()
    three = yz_v.at[pl.ds(0, 3)]
    pltpu.make_async_copy(three, three, y_s.at[1]).wait()
    for cp in outs + left_copies + last:
        cp.wait()


def reduce_call(act, ogq, ogkv, eq, ekv, bq, bkv):
    any_spec = pl.BlockSpec(memory_space=pl.ANY)
    hbm_spec = pl.BlockSpec(memory_space=pltpu.HBM)
    dma = pltpu.SemaphoreType.DMA
    v = pltpu.VMEM
    return pl.pallas_call(
        reduce_kernel,
        out_shape=[
            jax.ShapeDtypeStruct((CQ, D), BF16),
            jax.ShapeDtypeStruct((CQ, D), BF16),
            jax.ShapeDtypeStruct((D, 2 * CKV), BF16),
            jax.ShapeDtypeStruct((4 * RANK, D), BF16),
            jax.ShapeDtypeStruct((D, 4 * RANK), BF16),
            jax.ShapeDtypeStruct((CQ, 4 * RANK), BF16),
            jax.ShapeDtypeStruct((4 * RANK, CKV), BF16),
            jax.ShapeDtypeStruct((RANK, WIDE), F32),
        ],
        in_specs=[hbm_spec] * 7,
        out_specs=[any_spec] * 8,
        scratch_shapes=[
            v((SIDE, TOK, QUART), BF16),
            v((TOK, CKV), BF16),
            v((COLS, TOK), BF16),
            v((SIDE, CQ, QUART), BF16),
            v((SIDE, QUART, CKV), BF16),
            v((RANK, CQ), F32),
            v((RANK, CKV), F32),
            v((4 * RANK, TOK), BF16),
            v((2 * RANK, CQ), BF16),
            v((2 * RANK, CKV), BF16),
            v((SIDE, 2 * RANK, QUART), F32),
            v((SIDE, RANK, QUART), F32),
            v((SIDE, RANK, QUART), F32),
            v((SIDE * SIDE - 1, 8, QUART), F32),
            v((SIDE, 8, QUART), F32),
            v((SIDE, 2 * RANK, QUART), F32),
            v((SIDE, 4 * RANK, QUART), BF16),
            v((SIDE, 4 * RANK, QUART), BF16),
            v((SIDE, QUART, 4 * RANK), BF16),
            v((SIDE, CQ, QUART), BF16),
            v((SIDE, CQ, QUART), BF16),
            v((SIDE, QUART, 2 * CKV), BF16),
            v((RANK, WIDE), F32),
            v((16, WIDE), F32),
            v((SIDE, 16, WIDE), F32),
            v((RANK, WIDE), F32),
            v((2 * RANK, 128), F32),
            v((CQ, 4 * RANK), BF16),
            v((4 * RANK, CKV), BF16),
            v((RANK, WIDE), F32),
            dma((4,)), dma((SIDE, 3)),
            dma((SIDE,)), dma((SIDE,)),
            dma, dma, dma, dma,
            dma, dma((SIDE,)), dma((SIDE,)), dma((SIDE,)),
            dma((3,)), dma((3,)), dma((5, SIDE)),
        ],
        compiler_params=pltpu.CompilerParams(collective_id=0, has_side_effects=True, vmem_limit_bytes=40 * MIB),
        name="left_and_right_factors",
    )(act, ogq, ogkv, eq, ekv, bq, bkv)


def write_kernel(fqh, fqm, fkv, lq, tkv, zq, zkv, bn, uq, ukv, eq, ekv, bq, bkv):
    approx = mm(zq[...], lq[...])
    uq[...] = approx.astype(BF16)
    eq[0] = (fqh[...].astype(F32) + fqm[...].astype(F32) - approx).astype(BF16)
    approx = mm(tkv[...], zkv[...])
    ukv[...] = approx.astype(BF16)
    ekv[0] = (fkv[:, :CKV].astype(F32) + fkv[:, CKV:].astype(F32) - approx).astype(BF16)

    @pl.when(pl.program_id(0) == 0)
    def _():
        bkv[...] = bn[:, :CKV]
        bq[...] = bn[:, CKV:COLS]


def write_call(fqh, fqm, fkv, lq, tkv, zq, zkv, bn, step=640):
    by_row = lambda cols: pl.BlockSpec((step, cols), lambda i: (i, 0))
    by_lane = lambda rows: pl.BlockSpec((rows, step), lambda i: (0, i))
    whole = lambda *shape: pl.BlockSpec(shape, lambda i: (0,) * len(shape))
    return pl.pallas_call(
        write_kernel,
        grid=(D // step,),
        out_shape=[
            jax.ShapeDtypeStruct((CQ, D), BF16),
            jax.ShapeDtypeStruct((D, CKV), BF16),
            jax.ShapeDtypeStruct((1, CQ, D), BF16),
            jax.ShapeDtypeStruct((1, D, CKV), BF16),
            jax.ShapeDtypeStruct((RANK, CQ), F32),
            jax.ShapeDtypeStruct((RANK, CKV), F32),
        ],
        in_specs=[
            by_lane(CQ), by_lane(CQ), by_row(2 * CKV), by_lane(4 * RANK), by_row(4 * RANK),
            whole(CQ, 4 * RANK), whole(4 * RANK, CKV), whole(RANK, WIDE),
        ],
        out_specs=[
            by_lane(CQ),
            by_row(CKV),
            pl.BlockSpec((1, CQ, step), lambda i: (0, 0, i)),
            pl.BlockSpec((1, step, CKV), lambda i: (0, i, 0)),
            whole(RANK, CQ),
            whole(RANK, CKV),
        ],
        compiler_params=pltpu.CompilerParams(vmem_limit_bytes=24 * MIB),
        name="updates_and_errors",
    )(fqh, fqm, fkv, lq, tkv, zq, zkv, bn)


def local(act, ogq, ogkv, eq, ekv, bq, bkv):
    turned = lambda a: jnp.swapaxes(a, -1, -2)
    got = reduce_call(act, turned(ogq), ogkv, turned(eq), ekv, turned(bq), turned(bkv))
    uq, ukv, eq, ekv, bq, bkv = write_call(*got)
    return (turned(uq), ukv, turned(eq), ekv, turned(bq), turned(bkv))


def solution(mesh):
    placed = (
        P("dp", None, None),
        P("dp", None, "tensor"),
        P("dp", None, "tensor"),
        P("dp", None, "tensor"),
        P("dp", None, "tensor"),
        P("tensor", None),
        P("tensor", None),
    )
    return jax.shard_map(
        local,
        mesh=mesh,
        in_specs=placed,
        out_specs=(
            P(None, "tensor"),
            P(None, "tensor"),
            P("dp", None, "tensor"),
            P("dp", None, "tensor"),
            P("tensor", None),
            P("tensor", None),
        ),
        check_vma=False,
    )
```

time: 259 us -> 62.3 us (0.24)
  waiting for transfers between devices: 151 us -> 0 us
  Pallas kernels: 0 us -> 56.4 us
  matrix products: 50.2 us -> 0 us
  blocking collectives: 22.7 us -> 0 us
  other arithmetic: 14.6 us -> 0 us
  between operations: 14.3 us -> 0.65 us
    psum x1 -> x0, waiting for transfers between devices: 151 us -> none  [local(): left_both = lax.psum(local_left, ('dp', 'tensor'))]
    pallas_call x0 -> x2, Pallas kernels: none -> 56.4 us  [the longest x1 50.4 us: reduce_call(): pl.pallas_call(reduce_kernel, out_shape=[jax.ShapeDtypeStruct((CQ, D), BF...]
    dot_general x10 -> x0, matrix products: 46.4 us -> none  [the longest x2 11.6 us: weight_grad(): lax.dot_general(activations[0], out_grad[0], (((0,), (0,)), ((), ())), pr...]
    psum x1 -> x0, blocking collectives: 22.7 us -> none  [local(): summed_q, summed_kv = lax.psum((local_q, local_kv), 'dp')]
    another operation x10 -> x0, other arithmetic: 13.5 us -> none  [the longest x6 7.29 us: orthonormal(): lower = jnp.linalg.cholesky(gram)]
    another operation x2 -> x0, matrix products: 3.76 us -> none  [orthonormal(): lax.linalg.triangular_solve(lower, left, left_side=False, lower=True, tra...]
  transfers between devices with their start and end apart: 1 -> 0, of which waited for: 1 -> 0; matrix products, arithmetic and copies ran while one was open for 0% -> 0% of each run, Pallas kernels for 0% -> 0%
where the time goes in v1:
time: 62.3 us; the launch traced here: 62 us
  Pallas kernels  56.4 us (91%)
  local copies, waits for them, and re-layouts  4.86 us (8%)
  between operations  0.65 us (1%)
    pallas_call x1, Pallas kernels, reduce_call(): pl.pallas_call(reduce_kernel, out_shape=[jax.ShapeDtypeStruct((CQ, D), BF...  50.4 us
    pallas_call x1, Pallas kernels, write_call(): pl.pallas_call(write_kernel, grid=(D // step,), out_shape=[jax.ShapeDtype...  6.09 us
    unnamed x10, local copies, waits for them, and re-layouts  4.86 us

profile of v1, /device:TPU:1, one launch (start us, length us, event | category | flops | bytes accessed | tf_op | source)
XLA Modules:
  0.0 62.0 jit_solution(16584764773644503828)
XLA Ops:
  0.6 0.0 copy-start
  0.6 1.3 %copy-done = bf16[1,5120,128]{2,1,0:T(8,128)(2,1)S(1)} copy-done((bf16[1,5120,128]{2,1,0:T(8,128)(2,1)S(1)}, bf16[1,5120,128]{2,1,0:T(8,128)(2,1)}, u32[]{:S(2)}) %copy-start) | copy-done | bytes 1310744
  2.0 0.0 copy-start.1
  2.0 1.1 %copy-done.1 = bf16[1,1024,320]{1,2,0:T(8,128)(2,1)S(1)} copy-done((bf16[1,1024,320]{1,2,0:T(8,128)(2,1)S(1)}, bf16[1,1024,320]{1,2,0:T(8,128)(2,1)}, u32[]{:S(2)}) %copy-start.1) | copy-done | bytes 655384
  3.0 0.0 copy-start.2
  3.0 0.9 %copy-done.2 = bf16[1,1024,128]{2,1,0:T(8,128)(2,1)S(1)} copy-done((bf16[1,1024,128]{2,1,0:T(8,128)(2,1)S(1)}, bf16[1,1024,128]{2,1,0:T(8,128)(2,1)}, u32[]{:S(2)}) %copy-start.2) | copy-done | bytes 262168
  4.0 0.0 copy-start.3
  4.0 0.8 %copy-done.3 = f32[320,32]{0,1:T(8,128)S(1)} copy-done((f32[320,32]{0,1:T(8,128)S(1)}, f32[320,32]{0,1:T(8,128)}, u32[]{:S(2)}) %copy-start.3) | copy-done | bytes 40984
  4.8 0.0 copy-start.4
  4.8 0.7 %copy-done.4 = f32[128,32]{0,1:T(8,128)S(1)} copy-done((f32[128,32]{0,1:T(8,128)S(1)}, f32[128,32]{0,1:T(8,128)}, u32[]{:S(2)}) %copy-start.4) | copy-done | bytes 16408
  5.5 50.4 %left_and_right_factors.1 = (bf16[320,5120]{1,0:T(8,128)(2,1)S(1)}, bf16[320,5120]{1,0:T(8,128)(2,1)S(1)}, bf16[5120,256]{1,0:T(8,128)(2,1)S(1)}, bf16[128,5120]...) custom-call(bf16[1,1024,5120]{2,1,0:T(8,128)(2,1)} %act.1, ...), custom_call_target="tpu_custom_call" | custom-call | tf_op jit(solution)/shard_map/left_and_right_factors/pallas_call | solution.py:335
  55.9 6.1 %updates_and_errors.1 = (bf16[320,5120]{1,0:T(8,128)(2,1)}, bf16[5120,128]{1,0:T(8,128)(2,1)}, bf16[1,320,5120]{2,1,0:T(8,128)(2,1)}, bf16[1,5120,128]{2,1,0:T(8...) custom-call(bf16[320,5120]{1,0:T(8,128)(2,1)S(1)} %get-tuple-element.20.fqh, ...), custom_call_target="tpu_custom_call" | custom-call | tf_op jit(solution)/shard_map/updates_and_errors/pallas_call | solution.py:409
Async XLA Ops:
  0.6 1.3 %copy-start = (bf16[1,5120,128]{2,1,0:T(8,128)(2,1)S(1)}, bf16[1,5120,128]{2,1,0:T(8,128)(2,1)}, u32[]{:S(2)}) copy-start(bf16[1,5120,128]{2,1,0:T(8,128)(2,1)} %ekv.1) | copy-start | bytes 3932164
  2.0 1.1 %copy-start.1 = (bf16[1,1024,320]{1,2,0:T(8,128)(2,1)S(1)}, bf16[1,1024,320]{1,2,0:T(8,128)(2,1)}, u32[]{:S(2)}) copy-start(bf16[1,1024,320]{1,2,0:T(8,128)(2,1)} %param.8) | copy-start | bytes 1966084
  3.0 0.9 %copy-start.2 = (bf16[1,1024,128]{2,1,0:T(8,128)(2,1)S(1)}, bf16[1,1024,128]{2,1,0:T(8,128)(2,1)}, u32[]{:S(2)}) copy-start(bf16[1,1024,128]{2,1,0:T(8,128)(2,1)} %ogkv.1) | copy-start | bytes 786436
  4.0 0.8 %copy-start.3 = (f32[320,32]{0,1:T(8,128)S(1)}, f32[320,32]{0,1:T(8,128)}, u32[]{:S(2)}) copy-start(f32[320,32]{0,1:T(8,128)} %param.12) | copy-start | bytes 122884
  4.8 0.7 %copy-start.4 = (f32[128,32]{0,1:T(8,128)S(1)}, f32[128,32]{0,1:T(8,128)}, u32[]{:S(2)}) copy-start(f32[128,32]{0,1:T(8,128)} %param.13) | copy-start | bytes 49156

commit v2 on v0

v2 whole, which is shorter than its diff:
```python
import functools

import jax
import jax.numpy as jnp
from jax import lax
from jax.experimental import pallas as pl
from jax.experimental.pallas import tpu as pltpu
from jax.sharding import PartitionSpec as P

F32 = jnp.float32
BF16 = jnp.bfloat16
MESH = pl.DeviceIdType.MESH
HIGHEST = lax.Precision.HIGHEST
MIB = 1 << 20

SIDE = 4
D = 5120
WIDTHS = (768, 512)
STARTS = (0, SIDE * 768)
TOK = 1024
CQ, CKV = 320, 128
COLS = CQ + CKV
RANK = 32
WIDE = 512
ROT = (1, 3, 2, 0)
AG_ORDER = (0, 1, 3, 2)
UNITS = [(h, k) for h in range(2) for k in range(SIDE)]


def mm(a, b):
    return jnp.dot(a, b, preferred_element_type=F32)


def mm_t(a, b, precision=None):
    return lax.dot_general(a, b, (((1,), (1,)), ((), ())), preferred_element_type=F32, precision=precision)


def tmm(a, b, precision=None):
    return lax.dot_general(a, b, (((0,), (0,)), ((), ())), preferred_element_type=F32, precision=precision)


def halves(v):
    high = v.astype(BF16)
    return high, (v - high.astype(F32)).astype(BF16)


def eliminate(a, off):
    row = lax.broadcasted_iota(jnp.int32, (RANK, 128), 0)
    lane = lax.broadcasted_iota(jnp.int32, (RANK, 128), 1)
    for k in range(RANK - 1):
        col = jnp.broadcast_to(a[:, off + k : off + k + 1], (RANK, 128))
        scaled = a[k : k + 1, :] / col[k : k + 1, :]
        a = a - jnp.where(row > k, col, 0.0) * scaled
    diag = jnp.sum(jnp.where(lane == row + off, a, 0.0), axis=1, keepdims=True)
    return a * lax.rsqrt(diag)


def reduce_kernel(
    act, ogq, ogkv, eq, ekv, bq, bkv,
    fqh0, fqh1, fqm0, fqm1, fkv0, fkv1, lq0, lq1, tkv0, tkv1, zq_o, zkv_o, bn_o,
    act0, act1, eq0, eq1, ekv0, ekv1, loc0, loc1, xr0, xr1, sum0, sum1, rs0, rs1, zb0, zb1, lt0, lt1,
    ogkv_v, og_v, bq_v, bkv_v, pst_v, bq2_v, bkv2_v, yloc_v, yx_v, yz_v, ysum_v, gram_v,
    ld, lda, xs, xr, rs_s, rs_r, zs, zr, ag_s, ag_r, fw_s, fw_r, y_s, y_r,
):
    fqh, fqm, fkv, lq, tkv = (fqh0, fqh1), (fqm0, fqm1), (fkv0, fkv1), (lq0, lq1), (tkv0, tkv1)
    act_v, eq_v, ekv_v, loc_v, xr_v = (act0, act1), (eq0, eq1), (ekv0, ekv1), (loc0, loc1), (xr0, xr1)
    sum_v, rs_buf, zbuf, lt_v = (sum0, sum1), (rs0, rs1), (zb0, zb1), (lt0, lt1)

    dp, t = lax.axis_index("dp"), lax.axis_index("tensor")
    z, c = dp // 2, lax.rem(dp, 2)
    x, y = t // SIDE, lax.rem(t, SIDE)
    partner = (z * 2 + 1 - c, t)

    def plane(dx, dy):
        return (dp, lax.rem(x + dx, SIDE) * SIDE + lax.rem(y + dy, SIDE))

    def along_z(dz):
        return (lax.rem(z + dz, SIDE) * 2 + c, t)

    def part_of(rows, size):
        return pl.ds(pl.multiple_of(rows * size, size), size)

    def remote(src, dst, send, recv, device):
        return pltpu.make_async_remote_copy(
            src_ref=src, dst_ref=dst, send_sem=send, recv_sem=recv, device_id=device, device_id_type=MESH
        )

    def wait_for(ref, sem):
        pltpu.make_async_copy(ref, ref, sem).wait()

    def load(u):
        h, k = UNITS[u]
        g = lax.rem(x + ROT[k], SIDE)
        at = pl.ds(pl.multiple_of(STARTS[h] + g * WIDTHS[h], 256), WIDTHS[h])
        return [
            pltpu.make_async_copy(act.at[0, :, at], act_v[h].at[g], lda.at[u, 0]),
            pltpu.make_async_copy(eq.at[0, :, at], eq_v[h].at[g], lda.at[u, 1]),
            pltpu.make_async_copy(ekv.at[0, at, :], ekv_v[h].at[g], lda.at[u, 2]),
        ]

    first = [
        pltpu.make_async_copy(src, dst, ld.at[i])
        for i, (src, dst) in enumerate(
            [(ogq.at[0], og_v.at[pl.ds(CKV, CQ), :]), (ogkv.at[0], ogkv_v), (bq, bq_v), (bkv, bkv_v)]
        )
    ]
    for cp in first + load(0) + load(1):
        cp.start()

    barrier = pltpu.get_barrier_semaphore()
    peers = [partner]
    peers += [plane(dx, dy) for dx in range(SIDE) for dy in range(SIDE) if dx or dy]
    peers += [along_z(dz) for dz in (1, 2, 3)]
    for p in peers:
        pl.semaphore_signal(barrier, inc=1, device_id=p, device_id_type=MESH)

    for cp in first:
        cp.wait()
    og_v[:CKV, :] = jnp.transpose(ogkv_v[...])
    for src, b2, og_rows, base in ((bq_v, bq2_v, slice(CKV, COLS), 0), (bkv_v, bkv2_v, slice(0, CKV), 2 * RANK)):
        bt = src[...]
        high, mid = halves(bt)
        low = (bt - high.astype(F32) - mid.astype(F32)).astype(BF16)
        b2[:RANK, :] = high
        b2[RANK:, :] = mid
        og_w = og_v[og_rows, :]
        proj = mm(high, og_w) + (mm(mid, og_w) + mm(low, og_w))
        p_high, p_mid = halves(proj)
        pst_v[base : base + RANK, :] = p_high
        pst_v[base + RANK : base + 2 * RANK, :] = p_mid

    my_half, their_half = part_of(c, RANK), part_of(1 - c, RANK)

    def exchange(u):
        h, k = UNITS[u]
        return remote(loc_v[h].at[k, their_half, :], xr_v[h].at[k], xs.at[u], xr.at[u], partner)

    def scatter(u):
        h, k = UNITS[u]
        exchange(u).wait()
        sum_v[h][k] = loc_v[h][k, my_half, :] + xr_v[h][k]
        for dy in range(SIDE):
            if ROT[k] or dy:
                rows = part_of(lax.rem(y + dy, SIDE), 8)
                remote(
                    sum_v[h].at[k, rows, :], rs_buf[h].at[ROT[k] * SIDE + dy - 1], rs_s.at[h], rs_r.at[h],
                    plane(ROT[k], dy),
                ).start()

    for u, (h, k) in enumerate(UNITS):
        g = lax.rem(x + ROT[k], SIDE)
        for cp in load(u):
            cp.wait()
        if u + 2 < len(UNITS):
            for cp in load(u + 2):
                cp.start()
        bq2, bkv2 = bq2_v[...], bkv2_v[...]
        pst = pst_v[...]
        for i in range(WIDTHS[h] // 256):
            cut = slice(i * 256, (i + 1) * 256)
            prod = mm(pst, act_v[h][g, :, cut])
            from_q = mm(bq2, eq_v[h][g, :, cut])
            from_kv = mm_t(bkv2, ekv_v[h][g, cut, :])
            loc_v[h][k, :RANK, cut] = (prod[:RANK] + prod[RANK : 2 * RANK]) + (from_q[:RANK] + from_q[RANK:])
            loc_v[h][k, RANK:, cut] = (prod[2 * RANK : 3 * RANK] + prod[3 * RANK :]) + (from_kv[:RANK] + from_kv[RANK:])
        if u == 0:
            pl.semaphore_wait(barrier, len(peers))
        exchange(u).start()
        if u >= 1:
            scatter(u - 1)
    scatter(len(UNITS) - 1)

    def gradient(h, lo, hi):
        blocks = WIDTHS[h] // 256

        def body(i, _):
            g = i // blocks
            at = pl.ds(pl.multiple_of(lax.rem(i, blocks) * 256, 256), 256)
            grads = mm(og_v[...], act_v[h][g, :, at])
            high, mid = halves(jnp.transpose(grads[:CKV]) + ekv_v[h][g, at, :].astype(F32))
            fkv[h][g, at, :CKV] = high
            fkv[h][g, at, CKV:] = mid
            high, mid = halves(grads[CKV:] + eq_v[h][g, :, at].astype(F32))
            fqh[h][g, :, at] = high
            fqm[h][g, :, at] = mid
            return 0

        lax.fori_loop(lo * blocks, hi * blocks, body, 0)

    def sum_plane(h):
        wait_for(rs_buf[h], rs_r.at[h])
        part = sum_v[h][SIDE - 1, part_of(y, 8), :]
        for o in range(SIDE * SIDE - 1):
            part = part + rs_buf[h][o]
        zbuf[h][z] = part
        for dz in (1, 2, 3):
            remote(zbuf[h].at[z], zbuf[h].at[z], zs.at[h], zr.at[h], along_z(dz)).start()

    own = part_of(c * SIDE + y, 8)

    def gather(h):
        wait_for(zbuf[h].at[pl.ds(0, 3)], zr.at[h])
        lt_v[h][x, own, :] = (zbuf[h][0] + zbuf[h][1]) + (zbuf[h][2] + zbuf[h][3])
        for dx in AG_ORDER:
            for dy in range(SIDE):
                if dx or dy:
                    piece = lt_v[h].at[x, own, :]
                    remote(piece, piece, ag_s.at[h], ag_r.at[h * SIDE + x], plane(dx, dy)).start()

    gradient(0, 0, 1)
    sum_plane(0)
    gradient(0, 1, 3)
    sum_plane(1)
    gather(0)
    gradient(0, 3, 4)
    gradient(1, 0, 2)
    gather(1)
    gradient(1, 2, 4)

    def chunk_of(u):
        return lax.rem(x + AG_ORDER[u % SIDE], SIDE)

    def forward(u):
        piece = lt_v[u // SIDE].at[chunk_of(u), my_half, :]
        return remote(piece, piece, fw_s.at[u], fw_r.at[u], partner)

    def term(u, accs):
        h, g = u // SIDE, chunk_of(u)
        forward(u).wait()
        left = lt_v[h][g]
        high, mid = halves(left)
        q = jnp.concatenate([high[:RANK], mid[:RANK]], axis=0)
        kv = jnp.concatenate([high[RANK:], mid[RANK:]], axis=0)
        lq[h][g, : 2 * RANK, :] = q
        lq[h][g, 2 * RANK :, :] = q
        tkv[h][g] = jnp.transpose(jnp.concatenate([kv, kv], axis=0))
        return [
            accs[0] + mm_t(fqh[h][g], q),
            accs[1] + mm_t(fqm[h][g], high[:RANK]),
            accs[2] + mm(kv, fkv[h][g]),
            accs[3] + mm_t(left, left, precision=HIGHEST),
        ]

    accs = [
        jnp.zeros((CQ, 2 * RANK), F32),
        jnp.zeros((CQ, RANK), F32),
        jnp.zeros((2 * RANK, 2 * CKV), F32),
        jnp.zeros((2 * RANK, 2 * RANK), F32),
    ]
    for u in range(2 * SIDE):
        h = u // SIDE
        got = rs_buf[h].at[pl.ds(0, SIDE if AG_ORDER[u % SIDE] else SIDE - 1)]
        wait_for(got, ag_r.at[h * SIDE + chunk_of(u)])
        forward(u).start()
        if u >= 1:
            accs = term(u - 1, accs)
    accs = term(2 * SIDE - 1, accs)

    by_high = jnp.transpose(accs[0])
    yloc_v[:, CKV:COLS] = by_high[:RANK] + (by_high[RANK:] + jnp.transpose(accs[1]))
    yloc_v[:, :CKV] = accs[2][:RANK, :CKV] + (accs[2][RANK:, :CKV] + accs[2][:RANK, CKV:])
    yloc_v[:, COLS:] = jnp.zeros((RANK, WIDE - COLS), F32)

    my_rows, their_rows = part_of(c, 16), part_of(1 - c, 16)
    cp = remote(yloc_v.at[their_rows, :], yx_v, y_s.at[0], y_r.at[0], partner)
    cp.start()
    cp.wait()
    yz_v[z] = yloc_v[my_rows, :] + yx_v[...]
    for dz in (1, 2, 3):
        remote(yz_v.at[z], yz_v.at[z], y_s.at[1], y_r.at[1], along_z(dz)).start()

    gram_v[:, : 2 * RANK] = accs[3]
    gram_v[:, 2 * RANK :] = jnp.zeros((2 * RANK, 2 * RANK), F32)
    row = lax.broadcasted_iota(jnp.int32, (2 * RANK, 128), 0)
    lane = lax.broadcasted_iota(jnp.int32, (2 * RANK, 128), 1)
    same = (row < RANK) == (lane < RANK)
    aug = jnp.where(lane < 2 * RANK, jnp.where(same, gram_v[...], 0.0), jnp.where(lane == row + 2 * RANK, 1.0, 0.0))
    gram_v[:RANK, :] = eliminate(aug[:RANK], 0)
    gram_v[RANK:, :] = eliminate(aug[RANK:], RANK)
    inv = gram_v[:, 2 * RANK :]

    three = yz_v.at[pl.ds(0, 3)]
    wait_for(three, y_r.at[1])
    ysum_v[my_rows, :] = (yz_v[0] + yz_v[1]) + (yz_v[2] + yz_v[3])
    cp = remote(ysum_v.at[my_rows, :], ysum_v.at[my_rows, :], y_s.at[2], y_r.at[2], partner)
    cp.start()
    cp.wait()

    total = ysum_v[...]
    is_kv = lax.broadcasted_iota(jnp.int32, (RANK, WIDE), 1) < CKV
    both = jnp.concatenate([jnp.where(is_kv, 0.0, total), jnp.where(is_kv, total, 0.0)], axis=0)
    new_t = jnp.dot(inv, both, precision=HIGHEST, preferred_element_type=F32) * (1.0 / 8.0)
    factor = tmm(inv, new_t, precision=HIGHEST)
    bn_o[...] = new_t[:RANK] + new_t[RANK:]
    high, mid = halves(factor)
    stack = jnp.concatenate([high[:RANK], high[:RANK], mid[:RANK], mid[:RANK]], axis=0)
    zq_o[...] = jnp.transpose(stack[:, CKV:COLS])
    zkv_o[...] = jnp.concatenate([high[RANK:], high[RANK:], mid[RANK:], mid[RANK:]], axis=0)[:, :CKV]

    for h in range(2):
        wait_for(rs_buf[h], rs_s.at[h])
        wait_for(zbuf[h].at[pl.ds(0, 3)], zs.at[h])
        wait_for(rs_buf[h], ag_s.at[h])
    wait_for(three, y_s.at[1])


def reduce_call(*args):
    any_spec = pl.BlockSpec(memory_space=pl.ANY)
    vmem_spec = pl.BlockSpec(memory_space=pltpu.VMEM)
    dma = pltpu.SemaphoreType.DMA
    v = pltpu.VMEM
    pair = lambda shape, dtype: [v(tuple(w if n is None else n for n in shape), dtype) for w in WIDTHS]
    outs = [
        *pair((SIDE, CQ, None), BF16),
        *pair((SIDE, CQ, None), BF16),
        *pair((SIDE, None, 2 * CKV), BF16),
        *pair((SIDE, 4 * RANK, None), BF16),
        *pair((SIDE, None, 4 * RANK), BF16),
        v((CQ, 4 * RANK), BF16),
        v((4 * RANK, CKV), BF16),
        v((RANK, WIDE), F32),
    ]
    return pl.pallas_call(
        reduce_kernel,
        out_shape=[jax.ShapeDtypeStruct(o.shape, o.dtype) for o in outs],
        in_specs=[any_spec] * 7,
        out_specs=[vmem_spec] * len(outs),
        scratch_shapes=[
            *pair((SIDE, TOK, None), BF16),
            *pair((SIDE, CQ, None), BF16),
            *pair((SIDE, None, CKV), BF16),
            *pair((SIDE, 2 * RANK, None), F32),
            *pair((SIDE, RANK, None), F32),
            *pair((SIDE, RANK, None), F32),
            *pair((SIDE * SIDE - 1, 8, None), F32),
            *pair((SIDE, 8, None), F32),
            *pair((SIDE, 2 * RANK, None), F32),
            v((TOK, CKV), BF16),
            v((COLS, TOK), BF16),
            v((RANK, CQ), F32),
            v((RANK, CKV), F32),
            v((4 * RANK, TOK), BF16),
            v((2 * RANK, CQ), BF16),
            v((2 * RANK, CKV), BF16),
            v((RANK, WIDE), F32),
            v((16, WIDE), F32),
            v((SIDE, 16, WIDE), F32),
            v((RANK, WIDE), F32),
            v((2 * RANK, 128), F32),
            dma((4,)), dma((2 * SIDE, 3)),
            dma((2 * SIDE,)), dma((2 * SIDE,)),
            dma((2,)), dma((2,)), dma((2,)), dma((2,)),
            dma((2,)), dma((2 * SIDE,)), dma((2 * SIDE,)), dma((2 * SIDE,)),
            dma((3,)), dma((3,)),
        ],
        compiler_params=pltpu.CompilerParams(collective_id=0, has_side_effects=True, vmem_limit_bytes=40 * MIB),
        name="left_and_right_factors",
    )(*[pltpu.with_memory_space_constraint(a, pltpu.HBM) for a in args])


def write_kernel(
    fqh0, fqh1, fqm0, fqm1, fkv0, fkv1, lq0, lq1, tkv0, tkv1, zq, zkv, bn,
    uq, ukv, eq, ekv, bq, bkv,
    uq0, uq1, ukv0, ukv1, eq0, eq1, ekv0, ekv1, sem,
):
    halved = (
        (fqh0, fqm0, fkv0, lq0, tkv0, uq0, ukv0, eq0, ekv0),
        (fqh1, fqm1, fkv1, lq1, tkv1, uq1, ukv1, eq1, ekv1),
    )
    copies = []
    for h, (fqh, fqm, fkv, lq, tkv, uq_v, ukv_v, eq_v, ekv_v) in enumerate(halved):
        for g in range(SIDE):
            approx = mm(zq[...], lq[g])
            uq_v[g] = approx.astype(BF16)
            eq_v[g] = (fqh[g].astype(F32) + fqm[g].astype(F32) - approx).astype(BF16)
            approx = mm(tkv[g], zkv[...])
            ukv_v[g] = approx.astype(BF16)
            ekv_v[g] = (fkv[g, :, :CKV].astype(F32) + fkv[g, :, CKV:].astype(F32) - approx).astype(BF16)
            at = pl.ds(STARTS[h] + g * WIDTHS[h], WIDTHS[h])
            pairs = [(uq_v, uq.at[:, at]), (ukv_v, ukv.at[at, :]), (eq_v, eq.at[0, :, at]), (ekv_v, ekv.at[0, at, :])]
            for i, (src, dst) in enumerate(pairs):
                cp = pltpu.make_async_copy(src.at[g], dst, sem.at[h * SIDE + g, i])
                cp.start()
                copies.append(cp)
    bkv[...] = bn[:, :CKV]
    bq[...] = bn[:, CKV:COLS]
    for cp in copies:
        cp.wait()


def write_call(*args):
    vmem_spec = pl.BlockSpec(memory_space=pltpu.VMEM)
    any_spec = pl.BlockSpec(memory_space=pl.ANY)
    pair = lambda *shape: [pltpu.VMEM(tuple(w if n is None else n for n in shape), BF16) for w in WIDTHS]
    return pl.pallas_call(
        write_kernel,
        out_shape=[
            jax.ShapeDtypeStruct((CQ, D), BF16),
            jax.ShapeDtypeStruct((D, CKV), BF16),
            jax.ShapeDtypeStruct((1, CQ, D), BF16),
            jax.ShapeDtypeStruct((1, D, CKV), BF16),
            jax.ShapeDtypeStruct((RANK, CQ), F32),
            jax.ShapeDtypeStruct((RANK, CKV), F32),
        ],
        in_specs=[vmem_spec] * len(args),
        out_specs=[any_spec] * 4 + [vmem_spec] * 2,
        scratch_shapes=[
            *pair(SIDE, CQ, None),
            *pair(SIDE, None, CKV),
            *pair(SIDE, CQ, None),
            *pair(SIDE, None, CKV),
            pltpu.SemaphoreType.DMA((2 * SIDE, 4)),
        ],
        compiler_params=pltpu.CompilerParams(vmem_limit_bytes=24 * MIB),
        name="updates_and_errors",
    )(*args)


def local(act, ogq, ogkv, eq, ekv, bq, bkv):
    turned = lambda a: jnp.swapaxes(a, -1, -2)
    got = reduce_call(act, turned(ogq), ogkv, turned(eq), ekv, turned(bq), turned(bkv))
    uq, ukv, eq, ekv, bq, bkv = write_call(*got)
    return (turned(uq), ukv, turned(eq), ekv, turned(bq), turned(bkv))


def solution(mesh):
    placed = (
        P("dp", None, None),
        P("dp", None, "tensor"),
        P("dp", None, "tensor"),
        P("dp", None, "tensor"),
        P("dp", None, "tensor"),
        P("tensor", None),
        P("tensor", None),
    )
    return jax.shard_map(
        local,
        mesh=mesh,
        in_specs=placed,
        out_specs=(
            P(None, "tensor"),
            P(None, "tensor"),
            P("dp", None, "tensor"),
            P("dp", None, "tensor"),
            P("tensor", None),
            P("tensor", None),
        ),
        check_vma=False,
    )
```

time: 259 us -> 51.1 us (0.20); the launches traced: 256 us -> 50.9 us
  waiting for transfers between devices: 151 us -> 0 us
  Pallas kernels: 0 us -> 50.3 us
  matrix products: 50.2 us -> 0 us
  blocking collectives: 22.7 us -> 0 us
  other arithmetic: 14.6 us -> 0 us
  between operations: 14.3 us -> 0.64 us
  local copies, waits for them, and re-layouts: 2.89 us -> 0 us
    psum x1 -> x0, waiting for transfers between devices: 151 us -> none  [local(): left_both = lax.psum(local_left, ('dp', 'tensor'))]
    pallas_call x0 -> x2, Pallas kernels: none -> 50.3 us  [the longest x1 45.6 us: reduce_call(): pl.pallas_call(reduce_kernel, out_shape=[jax.ShapeDtypeStruct(o.shape, o....]
    dot_general x10 -> x0, matrix products: 46.4 us -> none  [the longest x2 11.6 us: weight_grad(): lax.dot_general(activations[0], out_grad[0], (((0,), (0,)), ((), ())), pr...]
    psum x1 -> x0, blocking collectives: 22.7 us -> none  [local(): summed_q, summed_kv = lax.psum((local_q, local_kv), 'dp')]
    another operation x10 -> x0, other arithmetic: 13.5 us -> none  [the longest x6 7.29 us: orthonormal(): lower = jnp.linalg.cholesky(gram)]
    another operation x2 -> x0, matrix products: 3.76 us -> none  [orthonormal(): lax.linalg.triangular_solve(lower, left, left_side=False, lower=True, tra...]
    unnamed x26 -> x0, local copies, waits for them, and re-layouts: 2.75 us -> none
  transfers between devices with their start and end apart: 1 -> 0, of which waited for: 1 -> 0; matrix products, arithmetic and copies ran while one was open for 0% -> 0% of each run, Pallas kernels for 0% -> 0%
where the time goes in v2:
time: 51.1 us; the launch traced here: 50.9 us
  Pallas kernels  50.3 us (98%)
  between operations  0.64 us (1%)
    pallas_call x1, Pallas kernels, reduce_call(): pl.pallas_call(reduce_kernel, out_shape=[jax.ShapeDtypeStruct(o.shape, o....  45.6 us
    pallas_call x1, Pallas kernels, write_call(): pl.pallas_call(write_kernel, out_shape=[jax.ShapeDtypeStruct((CQ, D), BF1...  4.7 us

profile of v2, /device:TPU:1, one launch (start us, length us, event | category | flops | bytes accessed | tf_op | source)
XLA Modules:
  0.0 50.9 jit_solution(17393155235177400561)
XLA Ops:
  0.6 45.6 %left_and_right_factors.1 = (bf16[4,320,768]{2,1,0:T(8,128)(2,1)S(1)}, bf16[4,320,512]{2,1,0:T(8,128)(2,1)S(1)}, bf16[4,320,768]{2,1,0:T(8,128)(2,1)S(1)}, bf16[...) custom-call(bf16[1,1024,5120]{2,1,0:T(8,128)(2,1)} %act.1, ...), custom_call_target="tpu_custom_call" | custom-call | tf_op jit(solution)/shard_map/left_and_right_factors/pallas_call | solution.py:323
  46.2 4.7 %updates_and_errors.1 = (bf16[320,5120]{1,0:T(8,128)(2,1)}, bf16[5120,128]{1,0:T(8,128)(2,1)}, bf16[1,320,5120]{2,1,0:T(8,128)(2,1)}, bf16[1,5120,128]{2,1,0:T(8...) custom-call(bf16[4,320,768]{2,1,0:T(8,128)(2,1)S(1)} %get-tuple-element.25.fqh0, ...), custom_call_target="tpu_custom_call" | custom-call | tf_op jit(solution)/shard_map/updates_and_errors/pallas_call | solution.py:395

commit v3 on v2

--- a/solution.py
+++ b/solution.py
@@ -15,8 +15,9 @@
 
 SIDE = 4
 D = 5120
-WIDTHS = (768, 512)
-STARTS = (0, SIDE * 768)
+WIDTHS = (512, 384, 384)
+PARTS = len(WIDTHS)
+STARTS = tuple(SIDE * sum(WIDTHS[:h]) for h in range(PARTS))
 TOK = 1024
 CQ, CKV = 320, 128
 COLS = CQ + CKV
@@ -24,7 +25,10 @@
 WIDE = 512
 ROT = (1, 3, 2, 0)
 AG_ORDER = (0, 1, 3, 2)
-UNITS = [(h, k) for h in range(2) for k in range(SIDE)]
+AHEAD = 3
+GATE = 4
+LAG = 2
+UNITS = [(h, k) for h in range(PARTS) for k in range(SIDE)]
 
 
 def mm(a, b):
@@ -55,27 +59,32 @@
     return a * lax.rsqrt(diag)
 
 
-def reduce_kernel(
-    act, ogq, ogkv, eq, ekv, bq, bkv,
-    fqh0, fqh1, fqm0, fqm1, fkv0, fkv1, lq0, lq1, tkv0, tkv1, zq_o, zkv_o, bn_o,
-    act0, act1, eq0, eq1, ekv0, ekv1, loc0, loc1, xr0, xr1, sum0, sum1, rs0, rs1, zb0, zb1, lt0, lt1,
-    ogkv_v, og_v, bq_v, bkv_v, pst_v, bq2_v, bkv2_v, yloc_v, yx_v, yz_v, ysum_v, gram_v,
-    ld, lda, xs, xr, rs_s, rs_r, zs, zr, ag_s, ag_r, fw_s, fw_r, y_s, y_r,
-):
-    fqh, fqm, fkv, lq, tkv = (fqh0, fqh1), (fqm0, fqm1), (fkv0, fkv1), (lq0, lq1), (tkv0, tkv1)
-    act_v, eq_v, ekv_v, loc_v, xr_v = (act0, act1), (eq0, eq1), (ekv0, ekv1), (loc0, loc1), (xr0, xr1)
-    sum_v, rs_buf, zbuf, lt_v = (sum0, sum1), (rs0, rs1), (zb0, zb1), (lt0, lt1)
+def by_part(refs, count):
+    return [refs[i * PARTS : (i + 1) * PARTS] for i in range(count)], refs[count * PARTS :]
+
+
+def reduce_kernel(act, ogq, ogkv, eq, ekv, bq, bkv, *refs):
+    (fqh, fqm, fkv, lq, tkv), refs = by_part(refs, 5)
+    zq_o, zkv_o, bn_o, *refs = refs
+    (act_v, eq_v, ekv_v, loc_v, xr_v, sum_v, rs_buf, zbuf, lt_v), refs = by_part(refs, 9)
+    ogkv_v, og_v, bq_v, bkv_v, pst_v, bq2_v, bkv2_v, yloc_v, yx_v, yz_v, ysum_v, gram_v, *refs = refs
+    ld, lda, xs, xr, rs_s, rs_r, zs, zr, ag_s, ag_r, fw_s, fw_r, y_s, y_r = refs
 
     dp, t = lax.axis_index("dp"), lax.axis_index("tensor")
     z, c = dp // 2, lax.rem(dp, 2)
     x, y = t // SIDE, lax.rem(t, SIDE)
     partner = (z * 2 + 1 - c, t)
 
-    def plane(dx, dy):
-        return (dp, lax.rem(x + dx, SIDE) * SIDE + lax.rem(y + dy, SIDE))
-
-    def along_z(dz):
-        return (lax.rem(z + dz, SIDE) * 2 + c, t)
+    spots = ((x, y, z), (y, z, x), (z, x, y))
+
+    def moved(d):
+        return (lax.rem(z + d[2], SIDE) * 2 + c, lax.rem(x + d[0], SIDE) * SIDE + lax.rem(y + d[1], SIDE))
+
+    def plane(h, d1, d2):
+        return moved(((d1, d2, 0), (0, d1, d2), (d2, 0, d1))[h])
+
+    def along(h, d):
+        return moved(((0, 0, d), (d, 0, 0), (0, d, 0))[h])
 
     def part_of(rows, size):
         return pl.ds(pl.multiple_of(rows * size, size), size)
@@ -90,12 +99,15 @@
 
     def load(u):
         h, k = UNITS[u]
-        g = lax.rem(x + ROT[k], SIDE)
-        at = pl.ds(pl.multiple_of(STARTS[h] + g * WIDTHS[h], 256), WIDTHS[h])
+        g = lax.rem(spots[h][0] + ROT[k], SIDE)
+        at = pl.ds(pl.multiple_of(STARTS[h] + g * WIDTHS[h], 128), WIDTHS[h])
+        return pltpu.make_async_copy(act.at[0, :, at], act_v[h].at[g], lda.at[u])
+
+    def load_errors(h):
+        at = pl.ds(STARTS[h], SIDE * WIDTHS[h])
         return [
-            pltpu.make_async_copy(act.at[0, :, at], act_v[h].at[g], lda.at[u, 0]),
-            pltpu.make_async_copy(eq.at[0, :, at], eq_v[h].at[g], lda.at[u, 1]),
-            pltpu.make_async_copy(ekv.at[0, at, :], ekv_v[h].at[g], lda.at[u, 2]),
+            pltpu.make_async_copy(eq.at[0, :, at], eq_v[h], ld.at[4 + 2 * h]),
+            pltpu.make_async_copy(ekv.at[0, at, :], ekv_v[h], ld.at[5 + 2 * h]),
         ]
 
     first = [
@@ -104,13 +116,14 @@
             [(ogq.at[0], og_v.at[pl.ds(CKV, CQ), :]), (ogkv.at[0], ogkv_v), (bq, bq_v), (bkv, bkv_v)]
         )
     ]
-    for cp in first + load(0) + load(1):
+    for cp in first + load_errors(0) + [load(u) for u in range(AHEAD)]:
         cp.start()
 
     barrier = pltpu.get_barrier_semaphore()
     peers = [partner]
-    peers += [plane(dx, dy) for dx in range(SIDE) for dy in range(SIDE) if dx or dy]
-    peers += [along_z(dz) for dz in (1, 2, 3)]
+    peers += [moved((i, j, 0)) for i in range(SIDE) for j in range(SIDE) if i or j]
+    peers += [moved((i, 0, j)) for i in range(SIDE) for j in (1, 2, 3)]
+    peers += [moved((0, i, j)) for i in (1, 2, 3) for j in (1, 2, 3)]
     for p in peers:
         pl.semaphore_signal(barrier, inc=1, device_id=p, device_id_type=MESH)
 
@@ -141,84 +154,94 @@
         sum_v[h][k] = loc_v[h][k, my_half, :] + xr_v[h][k]
         for dy in range(SIDE):
             if ROT[k] or dy:
-                rows = part_of(lax.rem(y + dy, SIDE), 8)
+                rows = part_of(lax.rem(spots[h][1] + dy, SIDE), 8)
                 remote(
                     sum_v[h].at[k, rows, :], rs_buf[h].at[ROT[k] * SIDE + dy - 1], rs_s.at[h], rs_r.at[h],
-                    plane(ROT[k], dy),
+                    plane(h, ROT[k], dy),
                 ).start()
 
     for u, (h, k) in enumerate(UNITS):
-        g = lax.rem(x + ROT[k], SIDE)
-        for cp in load(u):
-            cp.wait()
-        if u + 2 < len(UNITS):
-            for cp in load(u + 2):
+        g = lax.rem(spots[h][0] + ROT[k], SIDE)
+        load(u).wait()
+        if k == 0:
+            for cp in load_errors(h):
+                cp.wait()
+        if k == 1 and h + 1 < PARTS:
+            for cp in load_errors(h + 1):
                 cp.start()
+        for later in range(u + AHEAD, min(u + AHEAD + 1, len(UNITS)) if u < GATE else len(UNITS) if u == GATE else 0):
+            load(later).start()
         bq2, bkv2 = bq2_v[...], bkv2_v[...]
         pst = pst_v[...]
-        for i in range(WIDTHS[h] // 256):
-            cut = slice(i * 256, (i + 1) * 256)
-            prod = mm(pst, act_v[h][g, :, cut])
-            from_q = mm(bq2, eq_v[h][g, :, cut])
-            from_kv = mm_t(bkv2, ekv_v[h][g, cut, :])
-            loc_v[h][k, :RANK, cut] = (prod[:RANK] + prod[RANK : 2 * RANK]) + (from_q[:RANK] + from_q[RANK:])
-            loc_v[h][k, RANK:, cut] = (prod[2 * RANK : 3 * RANK] + prod[3 * RANK :]) + (from_kv[:RANK] + from_kv[RANK:])
-        if u == 0:
+        at = pl.ds(pl.multiple_of(g * WIDTHS[h], 128), WIDTHS[h])
+        prod = mm(pst, act_v[h][g])
+        from_q = mm(bq2, eq_v[h][:, at])
+        from_kv = mm_t(bkv2, ekv_v[h][at, :])
+        loc_v[h][k, :RANK, :] = (prod[:RANK] + prod[RANK : 2 * RANK]) + (from_q[:RANK] + from_q[RANK:])
+        loc_v[h][k, RANK:, :] = (prod[2 * RANK : 3 * RANK] + prod[3 * RANK :]) + (from_kv[:RANK] + from_kv[RANK:])
+        if u == GATE:
             pl.semaphore_wait(barrier, len(peers))
-        exchange(u).start()
-        if u >= 1:
-            scatter(u - 1)
-    scatter(len(UNITS) - 1)
+            for v in range(GATE):
+                exchange(v).start()
+        if u >= GATE:
+            exchange(u).start()
+        if u > GATE:
+            for v in range(max(0, u - LAG) if u > GATE + 1 else 0, u - LAG + 1):
+                scatter(v)
+    for v in range(len(UNITS) - LAG, len(UNITS)):
+        scatter(v)
 
     def gradient(h, lo, hi):
-        blocks = WIDTHS[h] // 256
-
-        def body(i, _):
-            g = i // blocks
-            at = pl.ds(pl.multiple_of(lax.rem(i, blocks) * 256, 256), 256)
-            grads = mm(og_v[...], act_v[h][g, :, at])
-            high, mid = halves(jnp.transpose(grads[:CKV]) + ekv_v[h][g, at, :].astype(F32))
-            fkv[h][g, at, :CKV] = high
-            fkv[h][g, at, CKV:] = mid
-            high, mid = halves(grads[CKV:] + eq_v[h][g, :, at].astype(F32))
-            fqh[h][g, :, at] = high
-            fqm[h][g, :, at] = mid
+        width = WIDTHS[h]
+
+        def body(g, _):
+            at = pl.ds(pl.multiple_of(g * width, width), width)
+            grads = mm(og_v[...], act_v[h][g])
+            high, mid = halves(jnp.transpose(grads[:CKV]) + ekv_v[h][at, :].astype(F32))
+            fkv[h][g, :, :CKV] = high
+            fkv[h][g, :, CKV:] = mid
+            high, mid = halves(grads[CKV:] + eq_v[h][:, at].astype(F32))
+            fqh[h][g] = high
+            fqm[h][g] = mid
             return 0
 
-        lax.fori_loop(lo * blocks, hi * blocks, body, 0)
+        lax.fori_loop(lo, hi, body, 0)
 
     def sum_plane(h):
         wait_for(rs_buf[h], rs_r.at[h])
-        part = sum_v[h][SIDE - 1, part_of(y, 8), :]
+        part = sum_v[h][SIDE - 1, part_of(spots[h][1], 8), :]
         for o in range(SIDE * SIDE - 1):
             part = part + rs_buf[h][o]
-        zbuf[h][z] = part
-        for dz in (1, 2, 3):
-            remote(zbuf[h].at[z], zbuf[h].at[z], zs.at[h], zr.at[h], along_z(dz)).start()
-
-    own = part_of(c * SIDE + y, 8)
+        here = spots[h][2]
+        zbuf[h][here] = part
+        for d in (1, 2, 3):
+            remote(zbuf[h].at[here], zbuf[h].at[here], zs.at[h], zr.at[h], along(h, d)).start()
 
     def gather(h):
         wait_for(zbuf[h].at[pl.ds(0, 3)], zr.at[h])
-        lt_v[h][x, own, :] = (zbuf[h][0] + zbuf[h][1]) + (zbuf[h][2] + zbuf[h][3])
-        for dx in AG_ORDER:
-            for dy in range(SIDE):
-                if dx or dy:
-                    piece = lt_v[h].at[x, own, :]
-                    remote(piece, piece, ag_s.at[h], ag_r.at[h * SIDE + x], plane(dx, dy)).start()
-
-    gradient(0, 0, 1)
+        g, own = spots[h][0], part_of(c * SIDE + spots[h][1], 8)
+        lt_v[h][g, own, :] = (zbuf[h][0] + zbuf[h][1]) + (zbuf[h][2] + zbuf[h][3])
+        for d1 in AG_ORDER:
+            for d2 in range(SIDE):
+                if d1 or d2:
+                    piece = lt_v[h].at[g, own, :]
+                    remote(piece, piece, ag_s.at[h], ag_r.at[h * SIDE + g], plane(h, d1, d2)).start()
+
+    gradient(0, 0, 2)
     sum_plane(0)
-    gradient(0, 1, 3)
+    gradient(0, 2, 3)
     sum_plane(1)
+    gradient(0, 3, 4)
     gather(0)
-    gradient(0, 3, 4)
+    sum_plane(2)
     gradient(1, 0, 2)
     gather(1)
     gradient(1, 2, 4)
+    gather(2)
+    gradient(2, 0, 2)
 
     def chunk_of(u):
-        return lax.rem(x + AG_ORDER[u % SIDE], SIDE)
+        return lax.rem(spots[u // SIDE][0] + AG_ORDER[u % SIDE], SIDE)
 
     def forward(u):
         piece = lt_v[u // SIDE].at[chunk_of(u), my_half, :]
@@ -238,23 +261,41 @@
             accs[0] + mm_t(fqh[h][g], q),
             accs[1] + mm_t(fqm[h][g], high[:RANK]),
             accs[2] + mm(kv, fkv[h][g]),
-            accs[3] + mm_t(left, left, precision=HIGHEST),
         ]
 
     accs = [
         jnp.zeros((CQ, 2 * RANK), F32),
         jnp.zeros((CQ, RANK), F32),
         jnp.zeros((2 * RANK, 2 * CKV), F32),
-        jnp.zeros((2 * RANK, 2 * RANK), F32),
     ]
-    for u in range(2 * SIDE):
+
+    def pass_on(u):
         h = u // SIDE
         got = rs_buf[h].at[pl.ds(0, SIDE if AG_ORDER[u % SIDE] else SIDE - 1)]
         wait_for(got, ag_r.at[h * SIDE + chunk_of(u)])
         forward(u).start()
-        if u >= 1:
-            accs = term(u - 1, accs)
-    accs = term(2 * SIDE - 1, accs)
+
+    def gram(h):
+        return sum(mm_t(lt_v[h][g], lt_v[h][g], precision=HIGHEST) for g in range(SIDE))
+
+    for u in range(SIDE):
+        pass_on(u)
+    gradient(2, 2, 4)
+    for u in range(SIDE):
+        accs = term(u, accs)
+    for u in range(SIDE, 2 * SIDE):
+        pass_on(u)
+    early = gram(0)
+    for u in range(SIDE, 2 * SIDE):
+        accs = term(u, accs)
+    pass_on(2 * SIDE)
+    pass_on(2 * SIDE + 1)
+    accs = term(2 * SIDE, accs)
+    pass_on(2 * SIDE + 2)
+    accs = term(2 * SIDE + 1, accs)
+    pass_on(2 * SIDE + 3)
+    accs = term(2 * SIDE + 2, accs)
+    accs = term(2 * SIDE + 3, accs)
 
     by_high = jnp.transpose(accs[0])
     yloc_v[:, CKV:COLS] = by_high[:RANK] + (by_high[RANK:] + jnp.transpose(accs[1]))
@@ -267,9 +308,9 @@
     cp.wait()
     yz_v[z] = yloc_v[my_rows, :] + yx_v[...]
     for dz in (1, 2, 3):
-        remote(yz_v.at[z], yz_v.at[z], y_s.at[1], y_r.at[1], along_z(dz)).start()
-
-    gram_v[:, : 2 * RANK] = accs[3]
+        remote(yz_v.at[z], yz_v.at[z], y_s.at[1], y_r.at[1], along(0, dz)).start()
+
+    gram_v[:, : 2 * RANK] = early + gram(1) + gram(2)
     gram_v[:, 2 * RANK :] = jnp.zeros((2 * RANK, 2 * RANK), F32)
     row = lax.broadcasted_iota(jnp.int32, (2 * RANK, 128), 0)
     lane = lax.broadcasted_iota(jnp.int32, (2 * RANK, 128), 1)
@@ -297,7 +338,7 @@
     zq_o[...] = jnp.transpose(stack[:, CKV:COLS])
     zkv_o[...] = jnp.concatenate([high[RANK:], high[RANK:], mid[RANK:], mid[RANK:]], axis=0)[:, :CKV]
 
-    for h in range(2):
+    for h in range(PARTS):
         wait_for(rs_buf[h], rs_s.at[h])
         wait_for(zbuf[h].at[pl.ds(0, 3)], zs.at[h])
         wait_for(rs_buf[h], ag_s.at[h])
@@ -327,8 +368,8 @@
         out_specs=[vmem_spec] * len(outs),
         scratch_shapes=[
             *pair((SIDE, TOK, None), BF16),
-            *pair((SIDE, CQ, None), BF16),
-            *pair((SIDE, None, CKV), BF16),
+            *[v((CQ, SIDE * w), BF16) for w in WIDTHS],
+            *[v((SIDE * w, CKV), BF16) for w in WIDTHS],
             *pair((SIDE, 2 * RANK, None), F32),
             *pair((SIDE, RANK, None), F32),
             *pair((SIDE, RANK, None), F32),
@@ -347,10 +388,10 @@
             v((SIDE, 16, WIDE), F32),
             v((RANK, WIDE), F32),
             v((2 * RANK, 128), F32),
-            dma((4,)), dma((2 * SIDE, 3)),
-            dma((2 * SIDE,)), dma((2 * SIDE,)),
-            dma((2,)), dma((2,)), dma((2,)), dma((2,)),
-            dma((2,)), dma((2 * SIDE,)), dma((2 * SIDE,)), dma((2 * SIDE,)),
+            dma((4 + 2 * PARTS,)), dma((SIDE * PARTS,)),
+            dma((SIDE * PARTS,)), dma((SIDE * PARTS,)),
+            dma((PARTS,)), dma((PARTS,)), dma((PARTS,)), dma((PARTS,)),
+            dma((PARTS,)), dma((SIDE * PARTS,)), dma((SIDE * PARTS,)), dma((SIDE * PARTS,)),
             dma((3,)), dma((3,)),
         ],
         compiler_params=pltpu.CompilerParams(collective_id=0, has_side_effects=True, vmem_limit_bytes=40 * MIB),
@@ -358,17 +399,12 @@
     )(*[pltpu.with_memory_space_constraint(a, pltpu.HBM) for a in args])
 
 
-def write_kernel(
-    fqh0, fqh1, fqm0, fqm1, fkv0, fkv1, lq0, lq1, tkv0, tkv1, zq, zkv, bn,
-    uq, ukv, eq, ekv, bq, bkv,
-    uq0, uq1, ukv0, ukv1, eq0, eq1, ekv0, ekv1, sem,
-):
-    halved = (
-        (fqh0, fqm0, fkv0, lq0, tkv0, uq0, ukv0, eq0, ekv0),
-        (fqh1, fqm1, fkv1, lq1, tkv1, uq1, ukv1, eq1, ekv1),
-    )
+def write_kernel(*refs):
+    parts, refs = by_part(refs, 5)
+    zq, zkv, bn, uq, ukv, eq, ekv, bq, bkv, *refs = refs
+    staged, (sem,) = by_part(refs, 4)
     copies = []
-    for h, (fqh, fqm, fkv, lq, tkv, uq_v, ukv_v, eq_v, ekv_v) in enumerate(halved):
+    for h, (fqh, fqm, fkv, lq, tkv, uq_v, ukv_v, eq_v, ekv_v) in enumerate(zip(*parts, *staged)):
         for g in range(SIDE):
             approx = mm(zq[...], lq[g])
             uq_v[g] = approx.astype(BF16)
@@ -409,7 +445,7 @@
             *pair(SIDE, None, CKV),
             *pair(SIDE, CQ, None),
             *pair(SIDE, None, CKV),
-            pltpu.SemaphoreType.DMA((2 * SIDE, 4)),
+            pltpu.SemaphoreType.DMA((SIDE * PARTS, 4)),
         ],
         compiler_params=pltpu.CompilerParams(vmem_limit_bytes=24 * MIB),
         name="updates_and_errors",

time: 51.1 us -> 50.4 us (0.986)
  Pallas kernels: 50.3 us -> 49.5 us
    pallas_call x1, Pallas kernels: 45.6 us -> 44.6 us  [reduce_call(): pl.pallas_call(reduce_kernel, out_shape=[jax.ShapeDtypeStruct(o.shape, o....]
where the time goes in v3:
time: 50.4 us; the launch traced here: 50.3 us
  Pallas kernels  49.5 us (98%)
  between operations  0.8 us (2%)
    pallas_call x1, Pallas kernels, reduce_call(): pl.pallas_call(reduce_kernel, out_shape=[jax.ShapeDtypeStruct(o.shape, o....  44.6 us
    pallas_call x1, Pallas kernels, write_call(): pl.pallas_call(write_kernel, out_shape=[jax.ShapeDtypeStruct((CQ, D), BF1...  4.82 us

profile of v3, /device:TPU:1, one launch (start us, length us, event | category | flops | bytes accessed | tf_op | source)
XLA Modules:
  0.0 50.3 jit_solution(5424395104259610312)
XLA Ops:
  0.6 44.6 %left_and_right_factors.1 = (bf16[4,320,512]{2,1,0:T(8,128)(2,1)S(1)}, bf16[4,320,384]{2,1,0:T(8,128)(2,1)S(1)}, bf16[4,320,384]{2,1,0:T(8,128)(2,1)S(1)}, bf16[...) custom-call(bf16[1,1024,5120]{2,1,0:T(8,128)(2,1)} %act.1, ...), custom_call_target="tpu_custom_call" | custom-call | tf_op jit(solution)/shard_map/left_and_right_factors/pallas_call | solution.py:364
  45.3 4.8 %updates_and_errors.1 = (bf16[320,5120]{1,0:T(8,128)(2,1)}, bf16[5120,128]{1,0:T(8,128)(2,1)}, bf16[1,320,5120]{2,1,0:T(8,128)(2,1)}, bf16[1,5120,128]{2,1,0:T(8...) custom-call(bf16[4,320,512]{2,1,0:T(8,128)(2,1)S(1)} %get-tuple-element.30.refs_0_, ...), custom_call_target="tpu_custom_call" | custom-call | tf_op jit(solution)/shard_map/updates_and_errors/pallas_call | solution.py:431

commit v4 on v3

--- a/solution.py
+++ b/solution.py
@@ -288,14 +288,10 @@
     early = gram(0)
     for u in range(SIDE, 2 * SIDE):
         accs = term(u, accs)
-    pass_on(2 * SIDE)
-    pass_on(2 * SIDE + 1)
-    accs = term(2 * SIDE, accs)
-    pass_on(2 * SIDE + 2)
-    accs = term(2 * SIDE + 1, accs)
-    pass_on(2 * SIDE + 3)
-    accs = term(2 * SIDE + 2, accs)
-    accs = term(2 * SIDE + 3, accs)
+    for u in range(2 * SIDE, 3 * SIDE):
+        pass_on(u)
+    for u in range(2 * SIDE, 3 * SIDE):
+        accs = term(u, accs)
 
     by_high = jnp.transpose(accs[0])
     yloc_v[:, CKV:COLS] = by_high[:RANK] + (by_high[RANK:] + jnp.transpose(accs[1]))

time: 50.4 us -> 49.7 us (0.986)
  Pallas kernels: 49.5 us -> 48.8 us
    pallas_call x1, Pallas kernels: 44.6 us -> 44 us  [reduce_call(): pl.pallas_call(reduce_kernel, out_shape=[jax.ShapeDtypeStruct(o.shape, o....]
where the time goes in v4:
time: 49.7 us; the launch traced here: 49.6 us
  Pallas kernels  48.8 us (98%)
  between operations  0.8 us (2%)
    pallas_call x1, Pallas kernels, reduce_call(): pl.pallas_call(reduce_kernel, out_shape=[jax.ShapeDtypeStruct(o.shape, o....  44 us
    pallas_call x1, Pallas kernels, write_call(): pl.pallas_call(write_kernel, out_shape=[jax.ShapeDtypeStruct((CQ, D), BF1...  4.82 us

profile of v4, /device:TPU:1, one launch (start us, length us, event | category | flops | bytes accessed | tf_op | source)
XLA Modules:
  0.0 49.6 jit_solution(18326778972220124939)
XLA Ops:
  0.6 44.0 %left_and_right_factors.1 = (bf16[4,320,512]{2,1,0:T(8,128)(2,1)S(1)}, bf16[4,320,384]{2,1,0:T(8,128)(2,1)S(1)}, bf16[4,320,384]{2,1,0:T(8,128)(2,1)S(1)}, bf16[...) custom-call(bf16[1,1024,5120]{2,1,0:T(8,128)(2,1)} %act.1, ...), custom_call_target="tpu_custom_call" | custom-call | tf_op jit(solution)/shard_map/left_and_right_factors/pallas_call | solution.py:360
  44.6 4.8 %updates_and_errors.1 = (bf16[320,5120]{1,0:T(8,128)(2,1)}, bf16[5120,128]{1,0:T(8,128)(2,1)}, bf16[1,320,5120]{2,1,0:T(8,128)(2,1)}, bf16[1,5120,128]{2,1,0:T(8...) custom-call(bf16[4,320,512]{2,1,0:T(8,128)(2,1)S(1)} %get-tuple-element.30.refs_0_, ...), custom_call_target="tpu_custom_call" | custom-call | tf_op jit(solution)/shard_map/updates_and_errors/pallas_call | solution.py:427

commit v5 on v4

--- a/solution.py
+++ b/solution.py
@@ -121,10 +121,11 @@
 
     barrier = pltpu.get_barrier_semaphore()
     peers = [partner]
-    peers += [moved((i, j, 0)) for i in range(SIDE) for j in range(SIDE) if i or j]
-    peers += [moved((i, 0, j)) for i in range(SIDE) for j in (1, 2, 3)]
-    peers += [moved((0, i, j)) for i in (1, 2, 3) for j in (1, 2, 3)]
-    for p in peers:
+    offsets = [(i, j, 0) for i in range(SIDE) for j in range(SIDE) if i or j]
+    offsets += [(i, 0, j) for i in range(SIDE) for j in (1, 2, 3)]
+    offsets += [(0, i, j) for i in (1, 2, 3) for j in (1, 2, 3)]
+    peers += [moved(d) for d in sorted(offsets, key=lambda d: sum(min(i, SIDE - i) for i in d))]
+    for p in reversed(peers):
         pl.semaphore_signal(barrier, inc=1, device_id=p, device_id_type=MESH)
 
     for cp in first:
@@ -247,16 +248,22 @@
         piece = lt_v[u // SIDE].at[chunk_of(u), my_half, :]
         return remote(piece, piece, fw_s.at[u], fw_r.at[u], partner)
 
+    def split_left(h, g):
+        high, mid = halves(lt_v[h][g])
+        q = jnp.concatenate([high[:RANK], mid[:RANK]], axis=0)
+        return high, q, jnp.concatenate([high[RANK:], mid[RANK:]], axis=0)
+
+    def hand_over(h, g, q, kv):
+        lq[h][g, : 2 * RANK, :] = q
+        lq[h][g, 2 * RANK :, :] = q
+        tkv[h][g] = jnp.transpose(jnp.concatenate([kv, kv], axis=0))
+
     def term(u, accs):
         h, g = u // SIDE, chunk_of(u)
         forward(u).wait()
-        left = lt_v[h][g]
-        high, mid = halves(left)
-        q = jnp.concatenate([high[:RANK], mid[:RANK]], axis=0)
-        kv = jnp.concatenate([high[RANK:], mid[RANK:]], axis=0)
-        lq[h][g, : 2 * RANK, :] = q
-        lq[h][g, 2 * RANK :, :] = q
-        tkv[h][g] = jnp.transpose(jnp.concatenate([kv, kv], axis=0))
+        high, q, kv = split_left(h, g)
+        if h < PARTS - 1:
+            hand_over(h, g, q, kv)
         return [
             accs[0] + mm_t(fqh[h][g], q),
             accs[1] + mm_t(fqm[h][g], high[:RANK]),
@@ -306,6 +313,8 @@
     for dz in (1, 2, 3):
         remote(yz_v.at[z], yz_v.at[z], y_s.at[1], y_r.at[1], along(0, dz)).start()
 
+    for g in range(SIDE):
+        hand_over(PARTS - 1, g, *split_left(PARTS - 1, g)[1:])
     gram_v[:, : 2 * RANK] = early + gram(1) + gram(2)
     gram_v[:, 2 * RANK :] = jnp.zeros((2 * RANK, 2 * RANK), F32)
     row = lax.broadcasted_iota(jnp.int32, (2 * RANK, 128), 0)

time: 49.7 us -> 49.8 us (level)
  no operation moved by 1% of the time
where the time goes in v5:
time: 49.8 us; the launch traced here: 49.7 us
  Pallas kernels  48.9 us (98%)
  between operations  0.8 us (2%)
    pallas_call x1, Pallas kernels, reduce_call(): pl.pallas_call(reduce_kernel, out_shape=[jax.ShapeDtypeStruct(o.shape, o....  44.1 us
    pallas_call x1, Pallas kernels, write_call(): pl.pallas_call(write_kernel, out_shape=[jax.ShapeDtypeStruct((CQ, D), BF1...  4.81 us

profile of v5, /device:TPU:1, one launch (start us, length us, event | category | flops | bytes accessed | tf_op | source)
XLA Modules:
  0.0 49.7 jit_solution(788443639136977058)
XLA Ops:
  0.6 44.1 %left_and_right_factors.1 = (bf16[4,320,512]{2,1,0:T(8,128)(2,1)S(1)}, bf16[4,320,384]{2,1,0:T(8,128)(2,1)S(1)}, bf16[4,320,384]{2,1,0:T(8,128)(2,1)S(1)}, bf16[...) custom-call(bf16[1,1024,5120]{2,1,0:T(8,128)(2,1)} %act.1, ...), custom_call_target="tpu_custom_call" | custom-call | tf_op jit(solution)/shard_map/left_and_right_factors/pallas_call | solution.py:369
  44.7 4.8 %updates_and_errors.1 = (bf16[320,5120]{1,0:T(8,128)(2,1)}, bf16[5120,128]{1,0:T(8,128)(2,1)}, bf16[1,320,5120]{2,1,0:T(8,128)(2,1)}, bf16[1,5120,128]{2,1,0:T(8...) custom-call(bf16[4,320,512]{2,1,0:T(8,128)(2,1)S(1)} %get-tuple-element.30.refs_0_, ...), custom_call_target="tpu_custom_call" | custom-call | tf_op jit(solution)/shard_map/updates_and_errors/pallas_call | solution.py:436
